TPU v7x, 512 devices: a whole 4x4x16 slice. The times are simulated.
512 devices in a mesh: lon: 64 (over z, y_hi, core), lat: 8 (over x, y_lo).
Axes of the slice: x: 4, y: 4 (y_hi: 2, y_lo: 2; y = y_hi * 2 + y_lo), z: 16, core: 2. Of those that a mesh axis runs over, the one named last changes fastest.
Arguments:
- field: float32 [2, 2048, 2048], P(None, 'lon', 'lat'), may hold values from -6 to 6
- offsets: int32 [2048], P('lat'), may hold values from 0 to 2047, as said below
- fraction: float32 [2048], P('lat'), may hold values from 0 to 1
- helm: float32 [2], replicated, may hold values from 4 to 32
Outputs:
- solution: float32 [2, 2048, 2048], P(None, 'lon', 'lat')
Inputs may be any that keep to these rules, and one draw needn't show every extreme that they name: `offsets`: each row's offset is a whole number of longitude points; some row needs the whole circle but one point, some row none.
All inputs are finite; a program needn't handle non-finite values.
Results may differ from a plain program's by a relative error of at most 0.00002.
Values sent between devices are 32-bit elements; how exact they have to be, the bound alone decides.
A program may use at most 64 MiB of HBM per device.

v0:
```python
import jax
import jax.numpy as jnp
from jax import lax
from jax.sharding import PartitionSpec as P

SMOOTH = 2
COARSE = 4


OMEGA = 0.8


def with_halo(cells, sides, width, closed):
    for axis, dim in sides:
        count = lax.axis_size(axis)
        ends = count if closed else count - 1
        head = lax.slice_in_dim(cells, 0, width, axis=dim)
        tail = lax.slice_in_dim(cells, cells.shape[dim] - width, cells.shape[dim], axis=dim)
        cells = jnp.concatenate(
            [
                lax.ppermute(tail, axis, [(i, (i + 1) % count) for i in range(ends)]),
                cells,
                lax.ppermute(head, axis, [((i + 1) % count, i) for i in range(ends)]),
            ],
            axis=dim,
        )
    return cells


def passed_along(shard, axis, by):
    count = lax.axis_size(axis)
    return lax.ppermute(shard, axis, [(i, (i + by) % count) for i in range(count)])


def zonal_pair(x):
    rim = with_halo(x, (("lon", 1),), 1, True)
    return rim[:, 2:, :] + rim[:, :-2, :]


def meridional_pair(x):
    rim = with_halo(x, (("lat", 2),), 1, False)
    return rim[:, :, 2:] + rim[:, :, :-2]


def relax(x, rhs, coef, pair):
    diag = 1.0 + 4.0 * coef
    applied = diag * x - coef * (zonal_pair(x) + pair(x))
    return x + OMEGA * (rhs - applied) / diag


def defect(x, rhs, coef, pair):
    diag = 1.0 + 4.0 * coef
    return rhs - (diag * x - coef * (zonal_pair(x) + pair(x)))


def restrict(x):
    lev, nlon, nlat = x.shape
    return x.reshape(lev, nlon // 2, 2, nlat // 2, 2).mean(axis=(2, 4))


def prolong(x):
    return jnp.repeat(jnp.repeat(x, 2, axis=1), 2, axis=2)


def per_device(field, offsets, fraction, helm):
    width = field.shape[1]
    circuit = lax.axis_size("lon")
    block_shift = offsets // width
    remain = offsets % width
    moved = field
    for bit in range((circuit - 1).bit_length()):
        hopped = passed_along(moved, "lon", 1 << bit)
        take = block_shift // (1 << bit) % 2 == 1
        moved = jnp.where(take[None, None, :], hopped, moved)
    before = passed_along(moved, "lon", 1)
    current = jnp.concatenate([before, moved], axis=1)
    for bit in range((width - 1).bit_length()):
        rolled = jnp.roll(current, 1 << bit, axis=1)
        pick = remain // (1 << bit) % 2 == 1
        current = jnp.where(pick[None, None, :], rolled, current)
    shifted = current[:, width:, :]
    rim = with_halo(shifted, (("lon", 1),), 2, True)
    s = fraction[None, None, :]
    w_one = -s * (s - 1.0) * (s - 2.0) / 6.0
    w_two = (s + 1.0) * (s - 1.0) * (s - 2.0) / 2.0
    w_three = -(s + 1.0) * s * (s - 2.0) / 2.0
    w_four = (s + 1.0) * s * (s - 1.0) / 6.0
    departure = (
        w_one * rim[:, 3 : width + 3]
        + w_two * rim[:, 2 : width + 2]
        + w_three * rim[:, 1 : width + 1]
        + w_four * rim[:, 0:width]
    )
    coef0 = helm[:, None, None]
    coef1 = coef0 / 4.0
    coef2 = coef0 / 16.0
    level0 = jnp.zeros_like(departure)
    for sweep in range(SMOOTH):
        level0 = relax(level0, departure, coef0, meridional_pair)
    rhs1 = restrict(defect(level0, departure, coef0, meridional_pair))
    level1 = jnp.zeros_like(rhs1)
    for sweep in range(SMOOTH):
        level1 = relax(level1, rhs1, coef1, meridional_pair)
    rhs2 = restrict(defect(level1, rhs1, coef1, meridional_pair))

    def coarse_pair(x):
        edge = with_halo(x, (("lat", 2),), 1, False)
        return edge[:, :, 2:] + edge[:, :, :-2]

    level2 = jnp.zeros_like(rhs2)
    for sweep in range(COARSE):
        level2 = relax(level2, rhs2, coef2, coarse_pair)
    level1 = level1 + prolong(level2)
    for sweep in range(SMOOTH):
        level1 = relax(level1, rhs1, coef1, meridional_pair)
    level0 = level0 + prolong(level1)
    for sweep in range(SMOOTH):
        level0 = relax(level0, departure, coef0, meridional_pair)
    return level0


def solution(mesh):
    return jax.shard_map(
        per_device,
        mesh=mesh,
        in_specs=(P(None, "lon", "lat"), P("lat"), P("lat"), P()),
        out_specs=P(None, "lon", "lat"),
        check_vma=False,
    )
```

profile of v0, /device:TPU:6, one launch (start us, length us, event | category | flops | bytes accessed | tf_op | source)
XLA Modules:
  0.0 364.8 jit_solution(10447962772458830312)
XLA Ops:
  3.7 14.8 %collective-permute-done = f32[2,32,256]{1,2,0:T(8,128)S(1)} collective-permute-done((f32[2,32,256]{1,2,0:T(8,128)S(1)}, f32[2,32,256]{1,2,0:T(8,128)S(1)}, u32[]{:S(2)}, u32[]{:S(2)}) %collective-permute-start) | collective-permute-done | bytes 65568 | tf_op jit(solution)/shard_map/ppermute | solution.py:32
  20.6 10.1 %collective-permute-done.1 = f32[2,32,256]{1,2,0:T(8,128)S(1)} collective-permute-done((f32[2,32,256]{1,2,0:T(8,128)S(1)}, f32[2,32,256]{1,2,0:T(8,128)S(1)}, u32[]{:S(2)}, u32[]{:S(2)}) %collective-permute-start.1) | collective-permute-done | bytes 65568 | tf_op jit(solution)/shard_map/ppermute | solution.py:32
  32.7 8.5 %collective-permute-done.2 = f32[2,32,256]{1,2,0:T(8,128)S(1)} collective-permute-done((f32[2,32,256]{1,2,0:T(8,128)S(1)}, f32[2,32,256]{1,2,0:T(8,128)S(1)}, u32[]{:S(2)}, u32[]{:S(2)}) %collective-permute-start.2) | collective-permute-done | bytes 65568 | tf_op jit(solution)/shard_map/ppermute | solution.py:32
  43.2 10.6 %collective-permute-done.3 = f32[2,32,256]{1,2,0:T(8,128)S(1)} collective-permute-done((f32[2,32,256]{1,2,0:T(8,128)S(1)}, f32[2,32,256]{1,2,0:T(8,128)S(1)}, u32[]{:S(2)}, u32[]{:S(2)}) %collective-permute-start.3) | collective-permute-done | bytes 65568 | tf_op jit(solution)/shard_map/ppermute | solution.py:32
  57.7 7.3 %collective-permute-start.9 = (f32[2,1,256]{1,2,0:T(8,128)S(1)}, f32[2,1,256]{1,2,0:T(8,128)S(1)}, u32[]{:S(2)}, u32[]{:S(2)}) collective-permute-start(f32[2,1,256]{1,2,0:T(8,128)S(1)} %broadcast.239), channel_id=1, source_target_pairs={{8,0},{16,8},{24,16},{32,24},{40,32},{48,40},{56,48},{64,56},{72,6... | collective-permute-start | bytes 6152 | tf_op jit(solution)/shard_map/ppermute | solution.py:23
  73.8 23.4 %collective-permute-start.5 = (f32[2,32,256]{1,2,0:T(8,128)S(1)}, f32[2,32,256]{1,2,0:T(8,128)S(1)}, u32[]{:S(2)}, u32[]{:S(2)}) collective-permute-start(f32[2,32,256]{1,2,0:T(8,128)S(1)} %broadcast_select_fusion.4), channel_id=1, source_target_pairs={{0,256},{8,264},{16,272},{24,280},{32,288},{40,296},{48,304},{56,3... | collective-permute-start | bytes 196616 | tf_op jit(solution)/shard_map/ppermute | solution.py:32
  97.3 17.3 %collective-permute-done.5 = f32[2,32,256]{1,2,0:T(8,128)S(1)} collective-permute-done((f32[2,32,256]{1,2,0:T(8,128)S(1)}, f32[2,32,256]{1,2,0:T(8,128)S(1)}, u32[]{:S(2)}, u32[]{:S(2)}) %collective-permute-start.5) | collective-permute-done | bytes 65568 | tf_op jit(solution)/shard_map/ppermute | solution.py:32
  116.8 9.2 %collective-permute-done.6 = f32[2,32,256]{1,2,0:T(8,128)S(1)} collective-permute-done((f32[2,32,256]{1,2,0:T(8,128)S(1)}, f32[2,32,256]{1,2,0:T(8,128)S(1)}, u32[]{:S(2)}, u32[]{:S(2)}) %collective-permute-start.6) | collective-permute-done | bytes 65568 | tf_op jit(solution)/shard_map/ppermute | solution.py:32
  133.6 7.4 %collective-permute-done.8 = f32[2,2,256]{1,2,0:T(8,128)S(1)} collective-permute-done((f32[2,2,256]{1,2,0:T(8,128)S(1)}, f32[2,2,256]{1,2,0:T(8,128)S(1)}, u32[]{:S(2)}, u32[]{:S(2)}) %collective-permute-start.8) | collective-permute-done | bytes 4128 | tf_op jit(solution)/shard_map/ppermute | solution.py:21
  146.2 4.5 %collective-permute-start.15 = (f32[2,32,1]{1,2,0:T(1,128)S(1)}, f32[2,32,1]{1,2,0:T(1,128)S(1)}, u32[]{:S(2)}, u32[]{:S(2)}) collective-permute-start(f32[2,32,1]{1,2,0:T(1,128)S(1)} %get-tuple-element.27), channel_id=1, source_target_pairs={{1,0},{2,1},{3,2},{4,3},{5,4},{6,5},{7,6},{9,8},{10,9},{11,10},{12... | collective-permute-start | bytes 776 | tf_op jit(solution)/shard_map/ppermute | solution.py:23
  157.4 6.1 %collective-permute-start.17 = (f32[2,1,256]{1,2,0:T(8,128)S(1)}, f32[2,1,256]{1,2,0:T(8,128)S(1)}, u32[]{:S(2)}, u32[]{:S(2)}) collective-permute-start(f32[2,1,256]{1,2,0:T(8,128)S(1)} %get-tuple-element.21), channel_id=1, source_target_pairs={{8,0},{16,8},{24,16},{32,24},{40,32},{48,40},{56,48},{64,56},{72,6... | collective-permute-start | bytes 6152 | tf_op jit(solution)/shard_map/ppermute | solution.py:23
  177.2 6.1 %collective-permute-start.21 = (f32[2,1,128]{2,1,0:T(1,128)S(1)}, f32[2,1,128]{2,1,0:T(1,128)S(1)}, u32[]{:S(2)}, u32[]{:S(2)}) collective-permute-start(f32[2,1,128]{2,1,0:T(1,128)S(1)} %broadcast.243), channel_id=1, source_target_pairs={{8,0},{16,8},{24,16},{32,24},{40,32},{48,40},{56,48},{64,56},{72,6... | collective-permute-start | bytes 3080 | tf_op jit(solution)/shard_map/ppermute | solution.py:23
  185.7 5.6 %reshape.64 = f32[2,16,2,128,2]{4,3,2,1,0:T(8,128)} reshape(f32[2,32,256]{2,1,0:T(8,128)S(1)} %copy.106) | data formatting | bytes 131072 | tf_op jit(solution)/shard_map/reshape | solution.py:58
  194.2 7.3 %collective-permute-start.25 = (f32[2,1,128]{2,1,0:T(1,128)S(1)}, f32[2,1,128]{2,1,0:T(1,128)S(1)}, u32[]{:S(2)}, u32[]{:S(2)}) collective-permute-start(f32[2,1,128]{2,1,0:T(1,128)S(1)} %get-tuple-element.43), channel_id=1, source_target_pairs={{8,0},{16,8},{24,16},{32,24},{40,32},{48,40},{56,48},{64,56},{72,6... | collective-permute-start | bytes 3080 | tf_op jit(solution)/shard_map/ppermute | solution.py:23
  213.8 7.0 %collective-permute-start.29 = (f32[2,1,128]{2,1,0:T(1,128)S(1)}, f32[2,1,128]{2,1,0:T(1,128)S(1)}, u32[]{:S(2)}, u32[]{:S(2)}) collective-permute-start(f32[2,1,128]{2,1,0:T(1,128)S(1)} %get-tuple-element.39), channel_id=1, source_target_pairs={{8,0},{16,8},{24,16},{32,24},{40,32},{48,40},{56,48},{64,56},{72,6... | collective-permute-start | bytes 3080 | tf_op jit(solution)/shard_map/ppermute | solution.py:23
  231.3 6.1 %collective-permute-start.33 = (f32[2,1,64]{2,1,0:T(1,128)S(1)}, f32[2,1,64]{2,1,0:T(1,128)S(1)}, u32[]{:S(2)}, u32[]{:S(2)}) collective-permute-start(f32[2,1,64]{2,1,0:T(1,128)S(1)} %broadcast.247), channel_id=1, source_target_pairs={{8,0},{16,8},{24,16},{32,24},{40,32},{48,40},{56,48},{64,56},{72,6... | collective-permute-start | bytes 1544 | tf_op jit(solution)/shard_map/ppermute | solution.py:23
  240.7 5.2 %collective-permute-done.34 = f32[2,1,64]{2,1,0:T(1,128)S(1)} collective-permute-done((f32[2,1,64]{2,1,0:T(1,128)S(1)}, f32[2,1,64]{2,1,0:T(1,128)S(1)}, u32[]{:S(2)}, u32[]{:S(2)}) %collective-permute-start.34) | collective-permute-done | bytes 544 | tf_op jit(solution)/shard_map/ppermute | solution.py:21
  256.3 4.5 %collective-permute-done.40 = f32[2,8,1]{2,1,0:T(8,128)S(1)} collective-permute-done((f32[2,8,1]{2,1,0:T(8,128)S(1)}, f32[2,8,1]{2,1,0:T(8,128)S(1)}, u32[]{:S(2)}, u32[]{:S(2)}) %collective-permute-start.40) | collective-permute-done | bytes 96 | tf_op jit(solution)/shard_map/ppermute | solution.py:21
  260.8 6.1 %collective-permute-start.41 = (f32[2,1,64]{2,1,0:T(1,128)S(1)}, f32[2,1,64]{2,1,0:T(1,128)S(1)}, u32[]{:S(2)}, u32[]{:S(2)}) collective-permute-start(f32[2,1,64]{2,1,0:T(1,128)S(1)} %get-tuple-element.51), channel_id=1, source_target_pairs={{8,0},{16,8},{24,16},{32,24},{40,32},{48,40},{56,48},{64,56},{72,6... | collective-permute-start | bytes 1544 | tf_op jit(solution)/shard_map/ppermute | solution.py:23
  277.4 6.1 %collective-permute-start.45 = (f32[2,1,64]{2,1,0:T(1,128)S(1)}, f32[2,1,64]{2,1,0:T(1,128)S(1)}, u32[]{:S(2)}, u32[]{:S(2)}) collective-permute-start(f32[2,1,64]{2,1,0:T(1,128)S(1)} %get-tuple-element.47), channel_id=1, source_target_pairs={{8,0},{16,8},{24,16},{32,24},{40,32},{48,40},{56,48},{64,56},{72,6... | collective-permute-start | bytes 1544 | tf_op jit(solution)/shard_map/ppermute | solution.py:23
  294.4 6.4 %collective-permute-start.49 = (f32[2,1,128]{2,1,0:T(1,128)S(1)}, f32[2,1,128]{2,1,0:T(1,128)S(1)}, u32[]{:S(2)}, u32[]{:S(2)}) collective-permute-start(f32[2,1,128]{2,1,0:T(1,128)S(1)} %get-tuple-element.35), channel_id=1, source_target_pairs={{8,0},{16,8},{24,16},{32,24},{40,32},{48,40},{56,48},{64,56},{72,6... | collective-permute-start | bytes 3080 | tf_op jit(solution)/shard_map/ppermute | solution.py:23
  311.4 6.1 %collective-permute-start.53 = (f32[2,1,128]{2,1,0:T(1,128)S(1)}, f32[2,1,128]{2,1,0:T(1,128)S(1)}, u32[]{:S(2)}, u32[]{:S(2)}) collective-permute-start(f32[2,1,128]{2,1,0:T(1,128)S(1)} %get-tuple-element.31), channel_id=1, source_target_pairs={{8,0},{16,8},{24,16},{32,24},{40,32},{48,40},{56,48},{64,56},{72,6... | collective-permute-start | bytes 3080 | tf_op jit(solution)/shard_map/ppermute | solution.py:23
  328.7 6.6 %collective-permute-start.57 = (f32[2,1,256]{1,2,0:T(8,128)S(1)}, f32[2,1,256]{1,2,0:T(8,128)S(1)}, u32[]{:S(2)}, u32[]{:S(2)}) collective-permute-start(f32[2,1,256]{1,2,0:T(8,128)S(1)} %get-tuple-element.17), channel_id=1, source_target_pairs={{8,0},{16,8},{24,16},{32,24},{40,32},{48,40},{56,48},{64,56},{72,6... | collective-permute-start | bytes 6152 | tf_op jit(solution)/shard_map/ppermute | solution.py:23
  347.0 5.4 %collective-permute-start.61 = (f32[2,1,256]{1,2,0:T(8,128)S(1)}, f32[2,1,256]{1,2,0:T(8,128)S(1)}, u32[]{:S(2)}, u32[]{:S(2)}) collective-permute-start(f32[2,1,256]{1,2,0:T(8,128)S(1)} %get-tuple-element.13), channel_id=1, source_target_pairs={{8,0},{16,8},{24,16},{32,24},{40,32},{48,40},{56,48},{64,56},{72,6... | collective-permute-start | bytes 6152 | tf_op jit(solution)/shard_map/ppermute | solution.py:23
  (192 shorter events, 165.9 us)
Async XLA Ops:
  1.0 17.5 %collective-permute-start = (f32[2,32,256]{1,2,0:T(8,128)S(1)}, f32[2,32,256]{1,2,0:T(8,128)S(1)}, u32[]{:S(2)}, u32[]{:S(2)}) collective-permute-start(f32[2,32,256]{1,2,0:T(8,128)S(1)} %copy.104), channel_id=1, source_target_pairs={{0,8},{8,16},{16,24},{24,32},{32,40},{40,48},{48,56},{56,64},{64,7... | collective-permute-start | bytes 196616 | tf_op jit(solution)/shard_map/ppermute | solution.py:32
  53.8 19.9 %collective-permute-start.4 = (f32[2,32,256]{1,2,0:T(8,128)S(1)}, f32[2,32,256]{1,2,0:T(8,128)S(1)}, u32[]{:S(2)}, u32[]{:S(2)}) collective-permute-start(f32[2,32,256]{1,2,0:T(8,128)S(1)} %broadcast_select_fusion.3), channel_id=1, source_target_pairs={{0,128},{8,136},{16,144},{24,152},{32,160},{40,168},{48,176},{56,1... | collective-permute-start | bytes 196616 | tf_op jit(solution)/shard_map/ppermute | solution.py:32
  55.8 76.6 %collective-permute-start.10 = (f32[2,1,256]{1,2,0:T(8,128)S(1)}, f32[2,1,256]{1,2,0:T(8,128)S(1)}, u32[]{:S(2)}, u32[]{:S(2)}) collective-permute-start(f32[2,1,256]{1,2,0:T(8,128)S(1)} %broadcast.239), channel_id=1, source_target_pairs={{0,8},{8,16},{16,24},{24,32},{32,40},{40,48},{48,56},{56,64},{64,7... | collective-permute-start | bytes 6152 | tf_op jit(solution)/shard_map/ppermute | solution.py:21
  57.7 74.6 %collective-permute-start.9 = (f32[2,1,256]{1,2,0:T(8,128)S(1)}, f32[2,1,256]{1,2,0:T(8,128)S(1)}, u32[]{:S(2)}, u32[]{:S(2)}) collective-permute-start(f32[2,1,256]{1,2,0:T(8,128)S(1)} %broadcast.239), channel_id=1, source_target_pairs={{8,0},{16,8},{24,16},{32,24},{40,32},{48,40},{56,48},{64,56},{72,6... | collective-permute-start | bytes 6152 | tf_op jit(solution)/shard_map/ppermute | solution.py:23
  65.0 64.8 %collective-permute-start.11 = (f32[2,32,1]{1,2,0:T(1,128)S(1)}, f32[2,32,1]{1,2,0:T(1,128)S(1)}, u32[]{:S(2)}, u32[]{:S(2)}) collective-permute-start(f32[2,32,1]{1,2,0:T(1,128)S(1)} %broadcast.240), channel_id=1, source_target_pairs={{1,0},{2,1},{3,2},{4,3},{5,4},{6,5},{7,6},{9,8},{10,9},{11,10},{12... | collective-permute-start | bytes 776 | tf_op jit(solution)/shard_map/ppermute | solution.py:23
  69.0 63.4 %collective-permute-start.12 = (f32[2,32,1]{1,2,0:T(1,128)S(1)}, f32[2,32,1]{1,2,0:T(1,128)S(1)}, u32[]{:S(2)}, u32[]{:S(2)}) collective-permute-start(f32[2,32,1]{1,2,0:T(1,128)S(1)} %broadcast.240), channel_id=1, source_target_pairs={{0,1},{1,2},{2,3},{3,4},{4,5},{5,6},{6,7},{8,9},{9,10},{10,11},{11... | collective-permute-start | bytes 776 | tf_op jit(solution)/shard_map/ppermute | solution.py:21
  73.8 40.7 %collective-permute-start.5 = (f32[2,32,256]{1,2,0:T(8,128)S(1)}, f32[2,32,256]{1,2,0:T(8,128)S(1)}, u32[]{:S(2)}, u32[]{:S(2)}) collective-permute-start(f32[2,32,256]{1,2,0:T(8,128)S(1)} %broadcast_select_fusion.4), channel_id=1, source_target_pairs={{0,256},{8,264},{16,272},{24,280},{32,288},{40,296},{48,304},{56,3... | collective-permute-start | bytes 196616 | tf_op jit(solution)/shard_map/ppermute | solution.py:32
  141.8 15.2 %collective-permute-start.13 = (f32[2,1,256]{1,2,0:T(8,128)S(1)}, f32[2,1,256]{1,2,0:T(8,128)S(1)}, u32[]{:S(2)}, u32[]{:S(2)}) collective-permute-start(f32[2,1,256]{1,2,0:T(8,128)S(1)} %get-tuple-element.25), channel_id=1, source_target_pairs={{8,0},{16,8},{24,16},{32,24},{40,32},{48,40},{56,48},{64,56},{72,6... | collective-permute-start | bytes 6152 | tf_op jit(solution)/shard_map/ppermute | solution.py:23
  157.4 25.9 %collective-permute-start.17 = (f32[2,1,256]{1,2,0:T(8,128)S(1)}, f32[2,1,256]{1,2,0:T(8,128)S(1)}, u32[]{:S(2)}, u32[]{:S(2)}) collective-permute-start(f32[2,1,256]{1,2,0:T(8,128)S(1)} %get-tuple-element.21), channel_id=1, source_target_pairs={{8,0},{16,8},{24,16},{32,24},{40,32},{48,40},{56,48},{64,56},{72,6... | collective-permute-start | bytes 6152 | tf_op jit(solution)/shard_map/ppermute | solution.py:23
  163.5 21.8 %collective-permute-start.18 = (f32[2,1,256]{1,2,0:T(8,128)S(1)}, f32[2,1,256]{1,2,0:T(8,128)S(1)}, u32[]{:S(2)}, u32[]{:S(2)}) collective-permute-start(f32[2,1,256]{1,2,0:T(8,128)S(1)} %get-tuple-element.22), channel_id=1, source_target_pairs={{0,8},{8,16},{16,24},{24,32},{32,40},{40,48},{48,56},{56,64},{64,7... | collective-permute-start | bytes 6152 | tf_op jit(solution)/shard_map/ppermute | solution.py:21
  171.3 22.7 %collective-permute-start.23 = (f32[2,16,1]{2,1,0:T(8,128)S(1)}, f32[2,16,1]{2,1,0:T(8,128)S(1)}, u32[]{:S(2)}, u32[]{:S(2)}) collective-permute-start(f32[2,16,1]{2,1,0:T(8,128)S(1)} %broadcast.244), channel_id=1, source_target_pairs={{1,0},{2,1},{3,2},{4,3},{5,4},{6,5},{7,6},{9,8},{10,9},{11,10},{12... | collective-permute-start | bytes 392 | tf_op jit(solution)/shard_map/ppermute | solution.py:23
  174.2 19.9 %collective-permute-start.24 = (f32[2,16,1]{2,1,0:T(8,128)S(1)}, f32[2,16,1]{2,1,0:T(8,128)S(1)}, u32[]{:S(2)}, u32[]{:S(2)}) collective-permute-start(f32[2,16,1]{2,1,0:T(8,128)S(1)} %broadcast.244), channel_id=1, source_target_pairs={{0,1},{1,2},{2,3},{3,4},{4,5},{5,6},{6,7},{8,9},{9,10},{10,11},{11... | collective-permute-start | bytes 392 | tf_op jit(solution)/shard_map/ppermute | solution.py:21
  177.2 16.9 %collective-permute-start.21 = (f32[2,1,128]{2,1,0:T(1,128)S(1)}, f32[2,1,128]{2,1,0:T(1,128)S(1)}, u32[]{:S(2)}, u32[]{:S(2)}) collective-permute-start(f32[2,1,128]{2,1,0:T(1,128)S(1)} %broadcast.243), channel_id=1, source_target_pairs={{8,0},{16,8},{24,16},{32,24},{40,32},{48,40},{56,48},{64,56},{72,6... | collective-permute-start | bytes 3080 | tf_op jit(solution)/shard_map/ppermute | solution.py:23
  194.2 19.5 %collective-permute-start.25 = (f32[2,1,128]{2,1,0:T(1,128)S(1)}, f32[2,1,128]{2,1,0:T(1,128)S(1)}, u32[]{:S(2)}, u32[]{:S(2)}) collective-permute-start(f32[2,1,128]{2,1,0:T(1,128)S(1)} %get-tuple-element.43), channel_id=1, source_target_pairs={{8,0},{16,8},{24,16},{32,24},{40,32},{48,40},{56,48},{64,56},{72,6... | collective-permute-start | bytes 3080 | tf_op jit(solution)/shard_map/ppermute | solution.py:23
  209.3 31.3 %collective-permute-start.35 = (f32[2,8,1]{2,1,0:T(8,128)S(1)}, f32[2,8,1]{2,1,0:T(8,128)S(1)}, u32[]{:S(2)}, u32[]{:S(2)}) collective-permute-start(f32[2,8,1]{2,1,0:T(8,128)S(1)} %broadcast.248), channel_id=1, source_target_pairs={{1,0},{2,1},{3,2},{4,3},{5,4},{6,5},{7,6},{9,8},{10,9},{11,10},{12... | collective-permute-start | bytes 200 | tf_op jit(solution)/shard_map/ppermute | solution.py:23
  213.8 23.6 %collective-permute-start.29 = (f32[2,1,128]{2,1,0:T(1,128)S(1)}, f32[2,1,128]{2,1,0:T(1,128)S(1)}, u32[]{:S(2)}, u32[]{:S(2)}) collective-permute-start(f32[2,1,128]{2,1,0:T(1,128)S(1)} %get-tuple-element.39), channel_id=1, source_target_pairs={{8,0},{16,8},{24,16},{32,24},{40,32},{48,40},{56,48},{64,56},{72,6... | collective-permute-start | bytes 3080 | tf_op jit(solution)/shard_map/ppermute | solution.py:23
  220.8 18.5 %collective-permute-start.30 = (f32[2,1,128]{2,1,0:T(1,128)S(1)}, f32[2,1,128]{2,1,0:T(1,128)S(1)}, u32[]{:S(2)}, u32[]{:S(2)}) collective-permute-start(f32[2,1,128]{2,1,0:T(1,128)S(1)} %get-tuple-element.40), channel_id=1, source_target_pairs={{0,8},{8,16},{16,24},{24,32},{32,40},{40,48},{48,56},{56,64},{64,7... | collective-permute-start | bytes 3080 | tf_op jit(solution)/shard_map/ppermute | solution.py:21
  246.0 14.8 %collective-permute-start.37 = (f32[2,1,64]{2,1,0:T(1,128)S(1)}, f32[2,1,64]{2,1,0:T(1,128)S(1)}, u32[]{:S(2)}, u32[]{:S(2)}) collective-permute-start(f32[2,1,64]{2,1,0:T(1,128)S(1)} %get-tuple-element.55), channel_id=1, source_target_pairs={{8,0},{16,8},{24,16},{32,24},{40,32},{48,40},{56,48},{64,56},{72,6... | collective-permute-start | bytes 1544 | tf_op jit(solution)/shard_map/ppermute | solution.py:23
  260.8 16.5 %collective-permute-start.41 = (f32[2,1,64]{2,1,0:T(1,128)S(1)}, f32[2,1,64]{2,1,0:T(1,128)S(1)}, u32[]{:S(2)}, u32[]{:S(2)}) collective-permute-start(f32[2,1,64]{2,1,0:T(1,128)S(1)} %get-tuple-element.51), channel_id=1, source_target_pairs={{8,0},{16,8},{24,16},{32,24},{40,32},{48,40},{56,48},{64,56},{72,6... | collective-permute-start | bytes 1544 | tf_op jit(solution)/shard_map/ppermute | solution.py:23
  277.4 16.7 %collective-permute-start.45 = (f32[2,1,64]{2,1,0:T(1,128)S(1)}, f32[2,1,64]{2,1,0:T(1,128)S(1)}, u32[]{:S(2)}, u32[]{:S(2)}) collective-permute-start(f32[2,1,64]{2,1,0:T(1,128)S(1)} %get-tuple-element.47), channel_id=1, source_target_pairs={{8,0},{16,8},{24,16},{32,24},{40,32},{48,40},{56,48},{64,56},{72,6... | collective-permute-start | bytes 1544 | tf_op jit(solution)/shard_map/ppermute | solution.py:23
  294.4 16.9 %collective-permute-start.49 = (f32[2,1,128]{2,1,0:T(1,128)S(1)}, f32[2,1,128]{2,1,0:T(1,128)S(1)}, u32[]{:S(2)}, u32[]{:S(2)}) collective-permute-start(f32[2,1,128]{2,1,0:T(1,128)S(1)} %get-tuple-element.35), channel_id=1, source_target_pairs={{8,0},{16,8},{24,16},{32,24},{40,32},{48,40},{56,48},{64,56},{72,6... | collective-permute-start | bytes 3080 | tf_op jit(solution)/shard_map/ppermute | solution.py:23
  311.4 16.8 %collective-permute-start.53 = (f32[2,1,128]{2,1,0:T(1,128)S(1)}, f32[2,1,128]{2,1,0:T(1,128)S(1)}, u32[]{:S(2)}, u32[]{:S(2)}) collective-permute-start(f32[2,1,128]{2,1,0:T(1,128)S(1)} %get-tuple-element.31), channel_id=1, source_target_pairs={{8,0},{16,8},{24,16},{32,24},{40,32},{48,40},{56,48},{64,56},{72,6... | collective-permute-start | bytes 3080 | tf_op jit(solution)/shard_map/ppermute | solution.py:23
  328.7 16.9 %collective-permute-start.57 = (f32[2,1,256]{1,2,0:T(8,128)S(1)}, f32[2,1,256]{1,2,0:T(8,128)S(1)}, u32[]{:S(2)}, u32[]{:S(2)}) collective-permute-start(f32[2,1,256]{1,2,0:T(8,128)S(1)} %get-tuple-element.17), channel_id=1, source_target_pairs={{8,0},{16,8},{24,16},{32,24},{40,32},{48,40},{56,48},{64,56},{72,6... | collective-permute-start | bytes 6152 | tf_op jit(solution)/shard_map/ppermute | solution.py:23
  347.0 15.7 %collective-permute-start.61 = (f32[2,1,256]{1,2,0:T(8,128)S(1)}, f32[2,1,256]{1,2,0:T(8,128)S(1)}, u32[]{:S(2)}, u32[]{:S(2)}) collective-permute-start(f32[2,1,256]{1,2,0:T(8,128)S(1)} %get-tuple-element.13), channel_id=1, source_target_pairs={{8,0},{16,8},{24,16},{32,24},{40,32},{48,40},{56,48},{64,56},{72,6... | collective-permute-start | bytes 6152 | tf_op jit(solution)/shard_map/ppermute | solution.py:23
  (43 other events, 458.0 us)
where the time goes:
time: 367 us; the launch traced here: 365 us
  starting transfers between devices  230 us (63%)
  waiting for transfers between devices  114 us (31%)
  local copies, waits for them, and re-layouts  10.9 us (3%)
  other arithmetic  8.02 us (2%)
    ppermute x29, starting transfers between devices, with_halo(): lax.ppermute(head, axis, [((i + 1) % count, i) for i in range(ends)])  121 us
    ppermute x29, starting transfers between devices, with_halo(): lax.ppermute(tail, axis, [(i, (i + 1) % count) for i in range(ends)])  74.2 us
    ppermute x7, waiting for transfers between devices, passed_along(): lax.ppermute(shard, axis, [(i, (i + by) % count) for i in range(count)])  73.3 us
    ppermute x29, waiting for transfers between devices, with_halo(): lax.ppermute(tail, axis, [(i, (i + 1) % count) for i in range(ends)])  38.5 us
    ppermute x7, starting transfers between devices, passed_along(): lax.ppermute(shard, axis, [(i, (i + by) % count) for i in range(count)])  34.9 us
  transfers between devices with their start and end apart: 65, of which 22 were waited for; matrix products, arithmetic and copies ran while one was open for 4% of the time, Pallas kernels for 0%

commit v1 on v0

v1 whole, which is shorter than its diff:
```python
import jax
import jax.numpy as jnp
from jax import lax
from jax.experimental import pallas as pl
from jax.experimental.pallas import tpu as pltpu
from jax.sharding import PartitionSpec as P

MESH = pl.DeviceIdType.MESH
NLONDEV = 64
NLATDEV = 8
LANES = 128


def roll(x, shift):
    return pltpu.roll(x, shift % LANES, 1)


def lane_iota(rows):
    return lax.broadcasted_iota(jnp.int32, (rows, LANES), 1)


def sub_iota():
    return lax.broadcasted_iota(jnp.int32, (8, LANES), 0)


def pack_field(half):
    low = lane_iota(16) < 64
    pieces = []
    for chunk in range(4):
        for lev in range(2):
            first, second = half(lev, 0, chunk // 2), half(lev, 1, chunk // 2)
            if chunk % 2 == 0:
                pieces.append(jnp.where(low, first, roll(second, 64)))
            else:
                pieces.append(jnp.where(low, roll(first, 64), second))
    return jnp.concatenate(pieces, axis=0)


def by_chunk(values, dtype):
    chunk = sub_iota() // 2
    full = jnp.full((8, LANES), values[0], dtype)
    for c in range(1, 4):
        full = jnp.where(chunk == c, jnp.full((8, LANES), values[c], dtype), full)
    return full


def shift_rows(v, offset):
    coarse, fine = offset // 16, offset % 16
    for bit in range(7):
        take = (coarse // (1 << bit)) % 2 == 1
        v = [jnp.where(take, roll(x, 1 << bit), x) for x in v]
    for bit in range(4):
        by = 1 << bit
        take = (fine // by) % 2 == 1
        v = [jnp.where(take, v[r - by] if r >= by else roll(v[r - by + 16], 1), v[r]) for r in range(16)]
    return v


def interpolate(g, s):
    w_one = -s * (s - 1.0) * (s - 2.0) / 6.0
    w_two = (s + 1.0) * (s - 1.0) * (s - 2.0) / 2.0
    w_three = -(s + 1.0) * s * (s - 2.0) / 2.0
    w_four = (s + 1.0) * s * (s - 1.0) / 6.0
    ext = [roll(g[14], 1), roll(g[15], 1)] + g + [roll(g[0], -1)]
    return [w_one * ext[r + 3] + w_two * ext[r + 2] + w_three * ext[r + 1] + w_four * ext[r] for r in range(16)]


def exchange_kernel(field, offsets, fraction, ext, send1, recv1, send2, recv2, work,
                    sems, near_send, near_recv):
    d = lax.axis_index("lon")
    g = lax.axis_index("lat")
    north, south = g > 0, g < NLATDEV - 1

    barrier = pltpu.get_barrier_semaphore()

    def greet(j, carry):
        pl.semaphore_signal(barrier, inc=1, device_id={"lon": lax.rem(d + j, NLONDEV)}, device_id_type=MESH)
        return carry

    lax.fori_loop(1, NLONDEV, greet, 0)
    for there, to in ((north, -1), (south, 1)):
        @pl.when(there)
        def _():
            for dd in (-1, 0, 1):
                pl.semaphore_signal(
                    barrier, inc=1,
                    device_id={"lon": lax.rem(d + dd + NLONDEV, NLONDEV), "lat": g + to},
                    device_id_type=MESH)

    packed = pack_field(lambda lev, hi, pair: field[lev, 16 * hi:16 * hi + 16, 128 * pair:128 * pair + 128]).T
    for hi in range(2):
        send1[pl.ds(hi, 64, stride=2), :] = packed[64 * hi:64 * hi + 64]

    pl.semaphore_wait(barrier, NLONDEV - 1 + 3 * (north.astype(jnp.int32) + south.astype(jnp.int32)))

    def all_to_all(src, dst, which):
        mine = pl.ds(2 * d, 2)

        def send(j, carry):
            step = jnp.where(j % 2 == 0, 32 + j // 2, 31 - j // 2)
            peer = lax.rem(d + step, NLONDEV)
            pltpu.make_async_remote_copy(
                src_ref=src.at[pl.ds(2 * peer, 2)],
                dst_ref=dst.at[mine],
                send_sem=sems.at[2 * which],
                recv_sem=sems.at[2 * which + 1],
                device_id={"lon": peer},
                device_id_type=MESH,
            ).start()
            return carry

        lax.fori_loop(0, NLONDEV - 1, send, 0)
        pltpu.make_async_copy(src.at[mine], dst.at[mine], sems.at[2 * which + 1]).start()
        pltpu.make_async_copy(dst, dst, sems.at[2 * which + 1]).wait()

    def sent(src, which):
        part = src.at[pl.ds(0, 2 * NLONDEV - 2)]
        pltpu.make_async_copy(part, part, sems.at[2 * which]).wait()

    all_to_all(send1, recv1, 0)
    work[...] = recv1[...].T
    v = [work[pl.ds(r, 8, stride=16), :] for r in range(16)]
    own = [d + 64 * c for c in range(4)]
    v = shift_rows(v, by_chunk([offsets[i] for i in own], jnp.int32))
    v = interpolate(v, by_chunk([fraction[i] for i in own], jnp.float32))
    for r in range(16):
        work[pl.ds(r, 8, stride=16), :] = v[r]
    send2[...] = work[...].T
    all_to_all(send2, recv2, 1)
    ext[1, 32:160, :] = jnp.concatenate([recv2[pl.ds(hi, 64, stride=2), :] for hi in range(2)], axis=0).T

    def near(dd, to):
        if to == 0:
            src, dst = ext.at[1, pl.ds(32, 128)], ext.at[1 - dd, pl.ds(32, 128)]
        elif to < 0:
            src, dst = ext.at[1, pl.ds(32, 32)], ext.at[1 - dd, pl.ds(160, 32)]
        else:
            src, dst = ext.at[1, pl.ds(128, 32)], ext.at[1 - dd, pl.ds(0, 32)]
        return pltpu.make_async_remote_copy(
            src_ref=src, dst_ref=dst,
            send_sem=near_send.at[to + 1, dd + 1], recv_sem=near_recv.at[to + 1, dd + 1],
            device_id={"lon": lax.rem(d + dd + NLONDEV, NLONDEV), "lat": g + to},
            device_id_type=MESH)

    for dd in (-1, 1):
        near(dd, 0).start()
    for there, to in ((north, -1), (south, 1)):
        @pl.when(there)
        def _():
            for dd in (-1, 0, 1):
                near(dd, to).start()
    for edge, at in ((north, 0), (south, 160)):
        @pl.when(jnp.logical_not(edge))
        def _():
            for k in range(3):
                ext[k, at:at + 32, :] = jnp.zeros((32, LANES), jnp.float32)
    sent(send1, 0)
    sent(send2, 1)
    for dd in (-1, 1):
        near(dd, 0).wait()
    for there, to in ((north, -1), (south, 1)):
        @pl.when(there)
        def _():
            for dd in (-1, 0, 1):
                near(dd, to).wait_send()
                near(dd, -to).wait_recv()


def memo(f):
    seen = {}

    def g(i):
        if i not in seen:
            seen[i] = f(i)
        return seen[i]

    return g


def v_cycle(load, c0, inside):
    lane = lane_iota(8)

    def coefs(c):
        diag = 1.0 + 4.0 * c
        beta = inside * (0.8 / diag)
        return diag, c * inside, beta, beta * c

    diag0, mult0, beta0, gamma0 = coefs(c0)
    diag1, mult1, beta1, gamma1 = coefs(c0 * 0.25)
    diag2, mult2, beta2, gamma2 = coefs(c0 * 0.0625)

    def pairs(x, step):
        def f(i):
            return (x(i - 1) + x(i + 1)) + (roll(x(i), step) + roll(x(i), -step))
        return f

    def second(first, gamma, step):
        s = pairs(first, step)
        return memo(lambda i: 1.2 * first(i) + gamma * s(i))

    def sweep(x, first, gamma, step):
        s = pairs(x, step)
        return memo(lambda i: (0.2 * x(i) + first(i)) + gamma * s(i))

    def defect(x, rhs, diag, mult, step):
        s = pairs(x, step)
        return memo(lambda i: (rhs(i) - diag * x(i)) + mult * s(i))

    def restrict(x, step):
        even = (lane // step) % 2 == 0

        def f(i):
            q = x(2 * i) + x(2 * i + 1)
            return 0.25 * (q + jnp.where(even, roll(q, -step), roll(q, step)))
        return memo(f)

    dep = memo(load)
    first0 = memo(lambda i: beta0 * dep(i))
    x0 = second(first0, gamma0, 1)
    rhs1 = restrict(defect(x0, dep, diag0, mult0, 1), 1)
    first1 = memo(lambda i: beta1 * rhs1(i))
    x1 = second(first1, gamma1, 2)
    rhs2 = restrict(defect(x1, rhs1, diag1, mult1, 2), 2)
    first2 = memo(lambda i: beta2 * rhs2(i))
    x2 = second(first2, gamma2, 4)
    x2 = sweep(x2, first2, gamma2, 4)
    x2 = sweep(x2, first2, gamma2, 4)
    y1 = memo(lambda i: x1(i) + x2(i >> 1))
    y1 = sweep(y1, first1, gamma1, 2)
    y1 = sweep(y1, first1, gamma1, 2)
    y0 = memo(lambda i: x0(i) + y1(i >> 1))
    y0 = sweep(y0, first0, gamma0, 1)
    return sweep(y0, first0, gamma0, 1)


def window(rows):
    lane = lane_iota(8)

    def load(i):
        k, hi, r = (i + 32) // 32, (i % 32) // 16, i % 16
        before, here, after = rows(k, r), rows(k, r + 32), rows(k, r + 64)
        if hi == 0:
            sides = roll(jnp.where(lane < 32, after, before), -32)
            return jnp.where((lane >= 32) & (lane < 96), roll(here, 32), sides)
        sides = roll(jnp.where(lane < 96, after, before), 32)
        return jnp.where((lane >= 32) & (lane < 96), roll(here, -32), sides)

    return load


def inside_of(g):
    chunk, lane = sub_iota() // 2, lane_iota(8)
    out = ((g == 0) & (chunk == 0) & (lane < 32)) | ((g == NLATDEV - 1) & (chunk == 3) & (lane >= 96))
    return jnp.where(out, 0.0, 1.0)


def cycle_kernel(ext, helm, out, rows):
    g = lax.axis_index("lat")
    lev = sub_iota() % 2
    c0 = jnp.where(lev == 0, jnp.full((8, LANES), helm[0], jnp.float32), jnp.full((8, LANES), helm[1], jnp.float32))
    result = v_cycle(window(lambda k, at: ext[k, pl.ds(at, 8, stride=16), :]), c0, inside_of(g))
    for i in range(32):
        rows[8 * i:8 * i + 8, :] = result(i)
    low = lane_iota(8) < 64
    for block in range(4):
        for lev in range(2):
            for pair in range(2):
                left = rows[pl.ds(64 * block + 4 * pair + lev, 8, stride=8), :]
                right = rows[pl.ds(64 * block + 4 * pair + 2 + lev, 8, stride=8), :]
                out[lev, 8 * block:8 * block + 8, 128 * pair:128 * pair + 128] = jnp.where(
                    low, roll(left, -32), roll(right, 32))


def per_device(field, offsets, fraction, helm):
    vmem = pl.BlockSpec(memory_space=pltpu.VMEM)
    smem = pl.BlockSpec(memory_space=pltpu.SMEM)
    square = pltpu.VMEM((LANES, LANES), jnp.float32)
    ext = pl.pallas_call(
        exchange_kernel,
        out_shape=jax.ShapeDtypeStruct((3, 192, LANES), jnp.float32),
        in_specs=[vmem, smem, smem],
        out_specs=vmem,
        scratch_shapes=[
            square, square, square, square, square,
            pltpu.SemaphoreType.DMA((4,)),
            pltpu.SemaphoreType.DMA((3, 3)),
            pltpu.SemaphoreType.DMA((3, 3)),
        ],
        compiler_params=pltpu.CompilerParams(collective_id=0, has_side_effects=True, vmem_limit_bytes=16 * 1024 * 1024),
    )(field, offsets, fraction)
    return pl.pallas_call(
        cycle_kernel,
        out_shape=jax.ShapeDtypeStruct(field.shape, jnp.float32),
        in_specs=[vmem, smem],
        out_specs=vmem,
        scratch_shapes=[pltpu.VMEM((256, LANES), jnp.float32)],
        compiler_params=pltpu.CompilerParams(vmem_limit_bytes=16 * 1024 * 1024),
    )(ext, helm)


def solution(mesh):
    return jax.shard_map(
        per_device,
        mesh=mesh,
        in_specs=(P(None, "lon", "lat"), P("lat"), P("lat"), P()),
        out_specs=P(None, "lon", "lat"),
        check_vma=False,
    )
```

time: 367 us -> 49.4 us (0.13)
  starting transfers between devices: 230 us -> 0 us
  waiting for transfers between devices: 114 us -> 0 us
  Pallas kernels: 0 us -> 46.3 us
  local copies, waits for them, and re-layouts: 10.9 us -> 2.2 us
  other arithmetic: 8.02 us -> 0 us
    ppermute x65 -> x0, starting transfers between devices: 230 us -> none  [the longest x29 121 us: with_halo(): lax.ppermute(head, axis, [((i + 1) % count, i) for i in range(ends)])]
    ppermute x65 -> x0, waiting for transfers between devices: 114 us -> none  [the longest x7 73.3 us: passed_along(): lax.ppermute(shard, axis, [(i, (i + by) % count) for i in range(count)])]
    pallas_call x0 -> x2, Pallas kernels: none -> 46.3 us  [the longest x1 41.1 us: per_device(): pl.pallas_call(exchange_kernel, out_shape=jax.ShapeDtypeStruct((3, 192, L...]
    reshape x5 -> x0, local copies, waits for them, and re-layouts: 6.82 us -> none  [the longest x2 6.58 us: restrict(): return x.reshape(lev, nlon // 2, 2, nlat // 2, 2).mean(axis=(2, 4))]
  transfers between devices with their start and end apart: 65 -> 0, of which waited for: 22 -> 0; matrix products, arithmetic and copies ran while one was open for 4% -> 0% of each run, Pallas kernels for 0% -> 0%
where the time goes in v1:
time: 49.4 us; the launch traced here: 48.5 us
  Pallas kernels  46.3 us (94%)
  local copies, waits for them, and re-layouts  2.2 us (4%)
    pallas_call x1, Pallas kernels, per_device(): pl.pallas_call(exchange_kernel, out_shape=jax.ShapeDtypeStruct((3, 192, L...  41.1 us
    pallas_call x1, Pallas kernels, per_device(): pl.pallas_call(cycle_kernel, out_shape=jax.ShapeDtypeStruct(field.shape,...  5.16 us
    unnamed x8, local copies, waits for them, and re-layouts  2.2 us

profile of v1, /device:TPU:6, one launch (start us, length us, event | category | flops | bytes accessed | tf_op | source)
XLA Modules:
  0.0 48.5 jit_solution(8504530680453243192)
XLA Ops:
  0.0 0.0 copy-start
  0.0 0.8 %copy-done = f32[2,32,256]{2,1,0:T(8,128)S(1)} copy-done((f32[2,32,256]{2,1,0:T(8,128)S(1)}, f32[2,32,256]{2,1,0:T(8,128)}, u32[]{:S(2)}) %copy-start) | copy-done | bytes 65560
  0.8 0.0 copy-start.1
  0.8 0.7 %copy-done.1 = s32[256]{0:T(256)S(1)} copy-done((s32[256]{0:T(256)S(1)}, s32[256]{0:T(256)}, u32[]{:S(2)}) %copy-start.1) | copy-done | bytes 1048
  1.5 0.0 copy-start.2
  1.5 0.7 %copy-done.2 = f32[256]{0:T(256)S(1)} copy-done((f32[256]{0:T(256)S(1)}, f32[256]{0:T(256)}, u32[]{:S(2)}) %copy-start.2) | copy-done | bytes 1048
  2.2 0.0 copy-start.3
  2.2 41.1 %shard_map.46.ext = f32[3,192,128]{2,1,0:T(8,128)S(1)} custom-call(f32[2,32,256]{2,1,0:T(8,128)S(1)} %copy-done, s32[256]{0:T(256)S(1)} %copy-done.1, f32[256]{0:T(256)S(1)} %copy-done.2), custom_call_target="tpu_custom_call" | custom-call | tf_op jit(solution)/shard_map/pallas_call | solution.py:278
  43.3 0.0 copy-done.3
  43.3 5.2 %shard_map.47 = f32[2,32,256]{2,1,0:T(8,128)} custom-call(f32[3,192,128]{2,1,0:T(8,128)S(1)} %shard_map.46.ext, f32[2]{0:T(128)S(1)} %copy-done.3), custom_call_target="tpu_custom_call" | custom-call | tf_op jit(solution)/shard_map/pallas_call | solution.py:291
Async XLA Ops:
  0.0 0.8 %copy-start = (f32[2,32,256]{2,1,0:T(8,128)S(1)}, f32[2,32,256]{2,1,0:T(8,128)}, u32[]{:S(2)}) copy-start(f32[2,32,256]{2,1,0:T(8,128)} %field.1) | copy-start | bytes 196612
  0.8 0.7 %copy-start.1 = (s32[256]{0:T(256)S(1)}, s32[256]{0:T(256)}, u32[]{:S(2)}) copy-start(s32[256]{0:T(256)} %offsets.1) | copy-start | bytes 3076
  1.5 0.7 %copy-start.2 = (f32[256]{0:T(256)S(1)}, f32[256]{0:T(256)}, u32[]{:S(2)}) copy-start(f32[256]{0:T(256)} %fraction.1) | copy-start | bytes 3076
  2.2 41.1 %copy-start.3 = (f32[2]{0:T(128)S(1)}, f32[2]{0:T(128)}, u32[]{:S(2)}) copy-start(f32[2]{0:T(128)} %helm.1) | copy-start | bytes 28

commit v2 on v1

--- a/solution.py
+++ b/solution.py
@@ -8,6 +8,8 @@
 MESH = pl.DeviceIdType.MESH
 NLONDEV = 64
 NLATDEV = 8
+OWNERS = 32
+REP = NLONDEV // OWNERS
 LANES = 128
 
 
@@ -65,19 +67,20 @@
     return [w_one * ext[r + 3] + w_two * ext[r + 2] + w_three * ext[r + 1] + w_four * ext[r] for r in range(16)]
 
 
-def exchange_kernel(field, offsets, fraction, ext, send1, recv1, send2, recv2, work,
-                    sems, near_send, near_recv):
+def exchange_kernel(field_in, offsets_in, fraction_in, ext, field, offsets, fraction, send1, recv1, send2, recv2, work,
+                    load_sems, sems, near_send, near_recv):
     d = lax.axis_index("lon")
     g = lax.axis_index("lat")
     north, south = g > 0, g < NLATDEV - 1
+    owner = d < OWNERS
+
+    loads = [pltpu.make_async_copy(src, dst, load_sems.at[i]) for i, (src, dst) in enumerate(
+        ((field_in, field), (offsets_in, offsets), (fraction_in, fraction)))]
+    for load in loads:
+        load.start()
 
     barrier = pltpu.get_barrier_semaphore()
 
-    def greet(j, carry):
-        pl.semaphore_signal(barrier, inc=1, device_id={"lon": lax.rem(d + j, NLONDEV)}, device_id_type=MESH)
-        return carry
-
-    lax.fori_loop(1, NLONDEV, greet, 0)
     for there, to in ((north, -1), (south, 1)):
         @pl.when(there)
         def _():
@@ -87,47 +90,70 @@
                     device_id={"lon": lax.rem(d + dd + NLONDEV, NLONDEV), "lat": g + to},
                     device_id_type=MESH)
 
+    @pl.when(owner)
+    def _():
+        def greet(j, carry):
+            pl.semaphore_signal(barrier, inc=1, device_id={"lon": lax.rem(d + j, NLONDEV)}, device_id_type=MESH)
+            return carry
+
+        lax.fori_loop(1, NLONDEV, greet, 0)
+
+    loads[0].wait()
     packed = pack_field(lambda lev, hi, pair: field[lev, 16 * hi:16 * hi + 16, 128 * pair:128 * pair + 128]).T
     for hi in range(2):
-        send1[pl.ds(hi, 64, stride=2), :] = packed[64 * hi:64 * hi + 64]
-
-    pl.semaphore_wait(barrier, NLONDEV - 1 + 3 * (north.astype(jnp.int32) + south.astype(jnp.int32)))
-
-    def all_to_all(src, dst, which):
-        mine = pl.ds(2 * d, 2)
-
-        def send(j, carry):
-            step = jnp.where(j % 2 == 0, 32 + j // 2, 31 - j // 2)
-            peer = lax.rem(d + step, NLONDEV)
-            pltpu.make_async_remote_copy(
-                src_ref=src.at[pl.ds(2 * peer, 2)],
-                dst_ref=dst.at[mine],
-                send_sem=sems.at[2 * which],
-                recv_sem=sems.at[2 * which + 1],
-                device_id={"lon": peer},
-                device_id_type=MESH,
-            ).start()
+        for s in range(REP):
+            at = 64 * hi + OWNERS * s
+            send1[s, pl.ds(hi, OWNERS, stride=2), :] = packed[at:at + OWNERS]
+
+    one = owner.astype(jnp.int32)
+    pl.semaphore_wait(barrier, OWNERS - one + 3 * (north.astype(jnp.int32) + south.astype(jnp.int32)))
+    mine = pl.ds(2 * d, 2)
+
+    def collect(j, carry):
+        to = lax.rem(d + j, OWNERS)
+        pltpu.make_async_remote_copy(
+            src_ref=send1.at[:, pl.ds(2 * to, 2)], dst_ref=recv1.at[:, mine],
+            send_sem=sems.at[0], recv_sem=sems.at[1],
+            device_id={"lon": to}, device_id_type=MESH,
+        ).start()
+        return carry
+
+    lax.fori_loop(one, OWNERS, collect, 0)
+    loads[1].wait()
+    loads[2].wait()
+
+    @pl.when(owner)
+    def _():
+        pltpu.make_async_copy(send1.at[:, mine], recv1.at[:, mine], sems.at[1]).start()
+        pltpu.make_async_copy(recv1, recv1, sems.at[1]).wait()
+        for s in range(REP):
+            work[s] = recv1[s].T
+            v = [work[s, pl.ds(r, 8, stride=16), :] for r in range(16)]
+            own = [d + OWNERS * s + 64 * c for c in range(4)]
+            v = shift_rows(v, by_chunk([offsets[i] for i in own], jnp.int32))
+            v = interpolate(v, by_chunk([fraction[i] for i in own], jnp.float32))
+            for r in range(16):
+                work[s, pl.ds(r, 8, stride=16), :] = v[r]
+            send2[s] = work[s].T
+
+        def spread(j, carry):
+            to = j - lax.rem(j, 4) + lax.rem(j + d, 4)
+
+            @pl.when(to != d)
+            def _():
+                pltpu.make_async_remote_copy(
+                    src_ref=send2.at[:, pl.ds(2 * to, 2)], dst_ref=recv2.at[:, mine],
+                    send_sem=sems.at[2], recv_sem=sems.at[3],
+                    device_id={"lon": to}, device_id_type=MESH,
+                ).start()
             return carry
 
-        lax.fori_loop(0, NLONDEV - 1, send, 0)
-        pltpu.make_async_copy(src.at[mine], dst.at[mine], sems.at[2 * which + 1]).start()
-        pltpu.make_async_copy(dst, dst, sems.at[2 * which + 1]).wait()
-
-    def sent(src, which):
-        part = src.at[pl.ds(0, 2 * NLONDEV - 2)]
-        pltpu.make_async_copy(part, part, sems.at[2 * which]).wait()
-
-    all_to_all(send1, recv1, 0)
-    work[...] = recv1[...].T
-    v = [work[pl.ds(r, 8, stride=16), :] for r in range(16)]
-    own = [d + 64 * c for c in range(4)]
-    v = shift_rows(v, by_chunk([offsets[i] for i in own], jnp.int32))
-    v = interpolate(v, by_chunk([fraction[i] for i in own], jnp.float32))
-    for r in range(16):
-        work[pl.ds(r, 8, stride=16), :] = v[r]
-    send2[...] = work[...].T
-    all_to_all(send2, recv2, 1)
-    ext[1, 32:160, :] = jnp.concatenate([recv2[pl.ds(hi, 64, stride=2), :] for hi in range(2)], axis=0).T
+        lax.fori_loop(0, NLONDEV, spread, 0)
+        pltpu.make_async_copy(send2.at[:, mine], recv2.at[:, mine], sems.at[3]).start()
+
+    pltpu.make_async_copy(recv2, recv2, sems.at[3]).wait()
+    ext[1, 32:160, :] = jnp.concatenate(
+        [recv2[s, pl.ds(hi, OWNERS, stride=2), :] for hi in range(2) for s in range(REP)], axis=0).T
 
     def near(dd, to):
         if to == 0:
@@ -154,8 +180,17 @@
         def _():
             for k in range(3):
                 ext[k, at:at + 32, :] = jnp.zeros((32, LANES), jnp.float32)
-    sent(send1, 0)
-    sent(send2, 1)
+
+    @pl.when(owner)
+    def _():
+        for src, i in ((send1, 0), (send2, 2)):
+            part = src.at[:, pl.ds(0, src.shape[1] - 2)]
+            pltpu.make_async_copy(part, part, sems.at[i]).wait()
+
+    @pl.when(jnp.logical_not(owner))
+    def _():
+        pltpu.make_async_copy(send1, send1, sems.at[0]).wait()
+
     for dd in (-1, 1):
         near(dd, 0).wait()
     for there, to in ((north, -1), (south, 1)):
@@ -274,14 +309,20 @@
 def per_device(field, offsets, fraction, helm):
     vmem = pl.BlockSpec(memory_space=pltpu.VMEM)
     smem = pl.BlockSpec(memory_space=pltpu.SMEM)
-    square = pltpu.VMEM((LANES, LANES), jnp.float32)
+    hbm = pl.BlockSpec(memory_space=pltpu.HBM)
+    parts = pltpu.VMEM((REP, 2 * OWNERS, LANES), jnp.float32)
+    circles = pltpu.VMEM((REP, LANES, LANES), jnp.float32)
     ext = pl.pallas_call(
         exchange_kernel,
         out_shape=jax.ShapeDtypeStruct((3, 192, LANES), jnp.float32),
-        in_specs=[vmem, smem, smem],
+        in_specs=[hbm, hbm, hbm],
         out_specs=vmem,
         scratch_shapes=[
-            square, square, square, square, square,
+            pltpu.VMEM(field.shape, jnp.float32),
+            pltpu.SMEM(offsets.shape, jnp.int32),
+            pltpu.SMEM(fraction.shape, jnp.float32),
+            parts, circles, circles, parts, circles,
+            pltpu.SemaphoreType.DMA((3,)),
             pltpu.SemaphoreType.DMA((4,)),
             pltpu.SemaphoreType.DMA((3, 3)),
             pltpu.SemaphoreType.DMA((3, 3)),

time: 49.4 us -> 50.8 us (1.028); the launches traced: 48.5 us -> 50.6 us
  Pallas kernels: 46.3 us -> 48.4 us
    pallas_call x1, Pallas kernels: 41.1 us -> 43.2 us  [per_device(): pl.pallas_call(exchange_kernel, out_shape=jax.ShapeDtypeStruct((3, 192, L...]
where the time goes in v2:
time: 50.8 us; the launch traced here: 50.6 us
  Pallas kernels  48.4 us (95%)
  local copies, waits for them, and re-layouts  2.2 us (4%)
    pallas_call x1, Pallas kernels, per_device(): pl.pallas_call(exchange_kernel, out_shape=jax.ShapeDtypeStruct((3, 192, L...  43.2 us
    pallas_call x1, Pallas kernels, per_device(): pl.pallas_call(cycle_kernel, out_shape=jax.ShapeDtypeStruct(field.shape,...  5.16 us
    unnamed x8, local copies, waits for them, and re-layouts  2.2 us

profile of v2, /device:TPU:6, one launch (start us, length us, event | category | flops | bytes accessed | tf_op | source)
XLA Modules:
  0.0 50.6 jit_solution(10262185735390461170)
XLA Ops:
  0.0 0.0 copy-start
  0.0 0.8 %copy-done = f32[2,32,256]{2,1,0:T(8,128)S(1)} copy-done((f32[2,32,256]{2,1,0:T(8,128)S(1)}, f32[2,32,256]{2,1,0:T(8,128)}, u32[]{:S(2)}) %copy-start) | copy-done | bytes 65560
  0.8 0.0 copy-start.1
  0.8 0.7 %copy-done.1 = s32[256]{0:T(256)S(1)} copy-done((s32[256]{0:T(256)S(1)}, s32[256]{0:T(256)}, u32[]{:S(2)}) %copy-start.1) | copy-done | bytes 1048
  1.5 0.0 copy-start.2
  1.5 0.7 %copy-done.2 = f32[256]{0:T(256)S(1)} copy-done((f32[256]{0:T(256)S(1)}, f32[256]{0:T(256)}, u32[]{:S(2)}) %copy-start.2) | copy-done | bytes 1048
  2.2 0.0 copy-start.3
  2.2 43.2 %shard_map.46.ext = f32[3,192,128]{2,1,0:T(8,128)S(1)} custom-call(f32[2,32,256]{2,1,0:T(8,128)S(1)} %copy-done, s32[256]{0:T(256)S(1)} %copy-done.1, f32[256]{0:T(256)S(1)} %copy-done.2), custom_call_target="tpu_custom_call" | custom-call | tf_op jit(solution)/shard_map/pallas_call | solution.py:315
  45.4 0.0 copy-done.3
  45.4 5.2 %shard_map.47 = f32[2,32,256]{2,1,0:T(8,128)} custom-call(f32[3,192,128]{2,1,0:T(8,128)S(1)} %shard_map.46.ext, f32[2]{0:T(128)S(1)} %copy-done.3), custom_call_target="tpu_custom_call" | custom-call | tf_op jit(solution)/shard_map/pallas_call | solution.py:332
Async XLA Ops:
  0.0 0.8 %copy-start = (f32[2,32,256]{2,1,0:T(8,128)S(1)}, f32[2,32,256]{2,1,0:T(8,128)}, u32[]{:S(2)}) copy-start(f32[2,32,256]{2,1,0:T(8,128)} %field_in.1) | copy-start | bytes 196612
  0.8 0.7 %copy-start.1 = (s32[256]{0:T(256)S(1)}, s32[256]{0:T(256)}, u32[]{:S(2)}) copy-start(s32[256]{0:T(256)} %offsets_in.1) | copy-start | bytes 3076
  1.5 0.7 %copy-start.2 = (f32[256]{0:T(256)S(1)}, f32[256]{0:T(256)}, u32[]{:S(2)}) copy-start(f32[256]{0:T(256)} %fraction_in.1) | copy-start | bytes 3076
  2.2 43.2 %copy-start.3 = (f32[2]{0:T(128)S(1)}, f32[2]{0:T(128)}, u32[]{:S(2)}) copy-start(f32[2]{0:T(128)} %helm.1) | copy-start | bytes 28

commit v3 on v2

--- a/solution.py
+++ b/solution.py
@@ -328,7 +328,7 @@
             pltpu.SemaphoreType.DMA((3, 3)),
         ],
         compiler_params=pltpu.CompilerParams(collective_id=0, has_side_effects=True, vmem_limit_bytes=16 * 1024 * 1024),
-    )(field, offsets, fraction)
+    )(*(pltpu.with_memory_space_constraint(a, pltpu.HBM) for a in (field, offsets, fraction)))
     return pl.pallas_call(
         cycle_kernel,
         out_shape=jax.ShapeDtypeStruct(field.shape, jnp.float32),

time: 50.8 us -> 48.4 us (0.953)
  local copies, waits for them, and re-layouts: 2.2 us -> 0.01 us
    unnamed x8 -> x2, local copies, waits for them, and re-layouts: 2.2 us -> 0.01 us
where the time goes in v3:
time: 48.4 us; the launch traced here: 48.3 us
  Pallas kernels  48.3 us (100%)
    pallas_call x1, Pallas kernels, per_device(): pl.pallas_call(exchange_kernel, out_shape=jax.ShapeDtypeStruct((3, 192, L...  43.1 us
    pallas_call x1, Pallas kernels, per_device(): pl.pallas_call(cycle_kernel, out_shape=jax.ShapeDtypeStruct(field.shape,...  5.15 us

profile of v3, /device:TPU:6, one launch (start us, length us, event | category | flops | bytes accessed | tf_op | source)
XLA Modules:
  0.0 48.3 jit_solution(11601695775118683356)
XLA Ops:
  0.0 0.0 copy-start
  0.0 43.1 %shard_map.46.ext = f32[3,192,128]{2,1,0:T(8,128)S(1)} custom-call(f32[2,32,256]{2,1,0:T(8,128)} %field_in.1, s32[256]{0:T(256)} %offsets_in.1, f32[256]{0:T(256)} %fraction_in.1), custom_call_target="tpu_custom_call" | custom-call | tf_op jit(solution)/shard_map/pallas_call | solution.py:315
  43.1 0.0 copy-done
  43.1 5.2 %shard_map.47 = f32[2,32,256]{2,1,0:T(8,128)} custom-call(f32[3,192,128]{2,1,0:T(8,128)S(1)} %shard_map.46.ext, f32[2]{0:T(128)S(1)} %copy-done), custom_call_target="tpu_custom_call" | custom-call | tf_op jit(solution)/shard_map/pallas_call | solution.py:332
Async XLA Ops:
  0.0 43.1 %copy-start = (f32[2]{0:T(128)S(1)}, f32[2]{0:T(128)}, u32[]{:S(2)}) copy-start(f32[2]{0:T(128)} %helm.1) | copy-start | bytes 28

commit v4 on v3

--- a/solution.py
+++ b/solution.py
@@ -8,7 +8,9 @@
 MESH = pl.DeviceIdType.MESH
 NLONDEV = 64
 NLATDEV = 8
-OWNERS = 32
+FIRST = 0
+PLANES = 4
+OWNERS = 4 * PLANES
 REP = NLONDEV // OWNERS
 LANES = 128
 
@@ -72,7 +74,8 @@
     d = lax.axis_index("lon")
     g = lax.axis_index("lat")
     north, south = g > 0, g < NLATDEV - 1
-    owner = d < OWNERS
+    rank = lax.rem(d + NLONDEV - 4 * FIRST, NLONDEV)
+    owner = rank < OWNERS
 
     loads = [pltpu.make_async_copy(src, dst, load_sems.at[i]) for i, (src, dst) in enumerate(
         ((field_in, field), (offsets_in, offsets), (fraction_in, fraction)))]
@@ -107,12 +110,13 @@
 
     one = owner.astype(jnp.int32)
     pl.semaphore_wait(barrier, OWNERS - one + 3 * (north.astype(jnp.int32) + south.astype(jnp.int32)))
-    mine = pl.ds(2 * d, 2)
+    mine, ranked = pl.ds(2 * d, 2), pl.ds(2 * rank, 2)
 
     def collect(j, carry):
-        to = lax.rem(d + j, OWNERS)
+        to_rank = lax.rem(rank + j, OWNERS)
+        to = lax.rem(to_rank + 4 * FIRST, NLONDEV)
         pltpu.make_async_remote_copy(
-            src_ref=send1.at[:, pl.ds(2 * to, 2)], dst_ref=recv1.at[:, mine],
+            src_ref=send1.at[:, pl.ds(2 * to_rank, 2)], dst_ref=recv1.at[:, mine],
             send_sem=sems.at[0], recv_sem=sems.at[1],
             device_id={"lon": to}, device_id_type=MESH,
         ).start()
@@ -124,12 +128,12 @@
 
     @pl.when(owner)
     def _():
-        pltpu.make_async_copy(send1.at[:, mine], recv1.at[:, mine], sems.at[1]).start()
+        pltpu.make_async_copy(send1.at[:, ranked], recv1.at[:, mine], sems.at[1]).start()
         pltpu.make_async_copy(recv1, recv1, sems.at[1]).wait()
         for s in range(REP):
             work[s] = recv1[s].T
             v = [work[s, pl.ds(r, 8, stride=16), :] for r in range(16)]
-            own = [d + OWNERS * s + 64 * c for c in range(4)]
+            own = [rank + OWNERS * s + 64 * c for c in range(4)]
             v = shift_rows(v, by_chunk([offsets[i] for i in own], jnp.int32))
             v = interpolate(v, by_chunk([fraction[i] for i in own], jnp.float32))
             for r in range(16):
@@ -137,19 +141,21 @@
             send2[s] = work[s].T
 
         def spread(j, carry):
-            to = j - lax.rem(j, 4) + lax.rem(j + d, 4)
+            k = j // 4 - PLANES
+            plane = jnp.where(k < 0, k + PLANES, jnp.where(k % 2 == 0, 15 - k // 2, PLANES + k // 2))
+            to = lax.rem(4 * (plane + FIRST) + lax.rem(j + d, 4), NLONDEV)
 
             @pl.when(to != d)
             def _():
                 pltpu.make_async_remote_copy(
-                    src_ref=send2.at[:, pl.ds(2 * to, 2)], dst_ref=recv2.at[:, mine],
+                    src_ref=send2.at[:, pl.ds(2 * to, 2)], dst_ref=recv2.at[:, ranked],
                     send_sem=sems.at[2], recv_sem=sems.at[3],
                     device_id={"lon": to}, device_id_type=MESH,
                 ).start()
             return carry
 
         lax.fori_loop(0, NLONDEV, spread, 0)
-        pltpu.make_async_copy(send2.at[:, mine], recv2.at[:, mine], sems.at[3]).start()
+        pltpu.make_async_copy(send2.at[:, mine], recv2.at[:, ranked], sems.at[3]).start()
 
     pltpu.make_async_copy(recv2, recv2, sems.at[3]).wait()
     ext[1, 32:160, :] = jnp.concatenate(
@@ -249,22 +255,27 @@
             return 0.25 * (q + jnp.where(even, roll(q, -step), roll(q, step)))
         return memo(f)
 
-    dep = memo(load)
-    first0 = memo(lambda i: beta0 * dep(i))
-    x0 = second(first0, gamma0, 1)
-    rhs1 = restrict(defect(x0, dep, diag0, mult0, 1), 1)
-    first1 = memo(lambda i: beta1 * rhs1(i))
-    x1 = second(first1, gamma1, 2)
-    rhs2 = restrict(defect(x1, rhs1, diag1, mult1, 2), 2)
-    first2 = memo(lambda i: beta2 * rhs2(i))
-    x2 = second(first2, gamma2, 4)
-    x2 = sweep(x2, first2, gamma2, 4)
-    x2 = sweep(x2, first2, gamma2, 4)
-    y1 = memo(lambda i: x1(i) + x2(i >> 1))
-    y1 = sweep(y1, first1, gamma1, 2)
-    y1 = sweep(y1, first1, gamma1, 2)
-    y0 = memo(lambda i: x0(i) + y1(i >> 1))
-    y0 = sweep(y0, first0, gamma0, 1)
+    def all_of(f, low, high):
+        for i in range(low, high + 1):
+            f(i)
+        return f
+
+    dep = all_of(memo(load), -26, 57)
+    first0 = all_of(memo(lambda i: beta0 * dep(i)), -26, 57)
+    x0 = all_of(second(first0, gamma0, 1), -25, 56)
+    rhs1 = all_of(restrict(all_of(defect(x0, dep, diag0, mult0, 1), -24, 55), 1), -12, 27)
+    first1 = all_of(memo(lambda i: beta1 * rhs1(i)), -12, 27)
+    x1 = all_of(second(first1, gamma1, 2), -11, 26)
+    rhs2 = all_of(restrict(all_of(defect(x1, rhs1, diag1, mult1, 2), -10, 25), 2), -5, 12)
+    first2 = all_of(memo(lambda i: beta2 * rhs2(i)), -5, 12)
+    x2 = all_of(second(first2, gamma2, 4), -4, 11)
+    x2 = all_of(sweep(x2, first2, gamma2, 4), -3, 10)
+    x2 = all_of(sweep(x2, first2, gamma2, 4), -2, 9)
+    y1 = all_of(memo(lambda i: x1(i) + x2(i >> 1)), -3, 18)
+    y1 = all_of(sweep(y1, first1, gamma1, 2), -2, 17)
+    y1 = all_of(sweep(y1, first1, gamma1, 2), -1, 16)
+    y0 = all_of(memo(lambda i: x0(i) + y1(i >> 1)), -2, 33)
+    y0 = all_of(sweep(y0, first0, gamma0, 1), -1, 32)
     return sweep(y0, first0, gamma0, 1)
 
 

time: 48.4 us -> 42.6 us (0.88)
  Pallas kernels: 48.3 us -> 42.4 us
    pallas_call x1, Pallas kernels: 43.1 us -> 39.7 us  [per_device(): pl.pallas_call(exchange_kernel, out_shape=jax.ShapeDtypeStruct((3, 192, L...]
    pallas_call x1, Pallas kernels: 5.15 us -> 2.7 us  [per_device(): pl.pallas_call(cycle_kernel, out_shape=jax.ShapeDtypeStruct(field.shape,...]
where the time goes in v4:
time: 42.6 us; the launch traced here: 42.4 us
  Pallas kernels  42.4 us (100%)
    pallas_call x1, Pallas kernels, per_device(): pl.pallas_call(exchange_kernel, out_shape=jax.ShapeDtypeStruct((3, 192, L...  39.7 us
    pallas_call x1, Pallas kernels, per_device(): pl.pallas_call(cycle_kernel, out_shape=jax.ShapeDtypeStruct(field.shape,...  2.7 us

profile of v4, /device:TPU:6, one launch (start us, length us, event | category | flops | bytes accessed | tf_op | source)
XLA Modules:
  0.0 42.4 jit_solution(9362741362886432645)
XLA Ops:
  0.0 0.0 copy-start
  0.0 39.7 %shard_map.46.ext = f32[3,192,128]{2,1,0:T(8,128)S(1)} custom-call(f32[2,32,256]{2,1,0:T(8,128)} %field_in.1, s32[256]{0:T(256)} %offsets_in.1, f32[256]{0:T(256)} %fraction_in.1), custom_call_target="tpu_custom_call" | custom-call | tf_op jit(solution)/shard_map/pallas_call | solution.py:326
  39.7 0.0 copy-done
  39.7 2.7 %shard_map.47 = f32[2,32,256]{2,1,0:T(8,128)} custom-call(f32[3,192,128]{2,1,0:T(8,128)S(1)} %shard_map.46.ext, f32[2]{0:T(128)S(1)} %copy-done), custom_call_target="tpu_custom_call" | custom-call | tf_op jit(solution)/shard_map/pallas_call | solution.py:343
Async XLA Ops:
  0.0 39.7 %copy-start = (f32[2]{0:T(128)S(1)}, f32[2]{0:T(128)}, u32[]{:S(2)}) copy-start(f32[2]{0:T(128)} %helm.1) | copy-start | bytes 28

commit v5 on v4

--- a/solution.py
+++ b/solution.py
@@ -40,22 +40,32 @@
     return jnp.concatenate(pieces, axis=0)
 
 
-def by_chunk(values, dtype):
-    chunk = sub_iota() // 2
+def by_chunk(chunk, values, dtype):
     full = jnp.full((8, LANES), values[0], dtype)
     for c in range(1, 4):
         full = jnp.where(chunk == c, jnp.full((8, LANES), values[c], dtype), full)
     return full
 
 
-def shift_rows(v, offset):
-    coarse, fine = offset // 16, offset % 16
+def shift_coarse(x, offset):
+    v = [x[8 * i:8 * i + 8] for i in range(16)]
+    sub = sub_iota()
     for bit in range(7):
-        take = (coarse // (1 << bit)) % 2 == 1
-        v = [jnp.where(take, roll(x, 1 << bit), x) for x in v]
+        by = 1 << bit
+        take = (offset // (16 * by)) % 2 == 1
+        if by < 8:
+            turned = [pltpu.roll(u, by, 0) for u in v]
+            moved = [jnp.where(sub < by, turned[i - 1], turned[i]) for i in range(16)]
+        else:
+            moved = [v[i - by // 8] for i in range(16)]
+        v = [jnp.where(take, m, u) for m, u in zip(moved, v)]
+    return jnp.concatenate(v, axis=0)
+
+
+def shift_fine(v, offset):
     for bit in range(4):
         by = 1 << bit
-        take = (fine // by) % 2 == 1
+        take = (offset // by) % 2 == 1
         v = [jnp.where(take, v[r - by] if r >= by else roll(v[r - by + 16], 1), v[r]) for r in range(16)]
     return v
 
@@ -70,7 +80,7 @@
 
 
 def exchange_kernel(field_in, offsets_in, fraction_in, ext, field, offsets, fraction, send1, recv1, send2, recv2, work,
-                    load_sems, sems, near_send, near_recv):
+                    load_sems, sems, near_send, near_recv, lat_in, may_near):
     d = lax.axis_index("lon")
     g = lax.axis_index("lat")
     north, south = g > 0, g < NLATDEV - 1
@@ -84,14 +94,11 @@
 
     barrier = pltpu.get_barrier_semaphore()
 
-    for there, to in ((north, -1), (south, 1)):
-        @pl.when(there)
-        def _():
-            for dd in (-1, 0, 1):
-                pl.semaphore_signal(
-                    barrier, inc=1,
-                    device_id={"lon": lax.rem(d + dd + NLONDEV, NLONDEV), "lat": g + to},
-                    device_id_type=MESH)
+    def tell_lat(sem):
+        for there, to in ((north, -1), (south, 1)):
+            @pl.when(there)
+            def _():
+                pl.semaphore_signal(sem, inc=1, device_id={"lat": g + to}, device_id_type=MESH)
 
     @pl.when(owner)
     def _():
@@ -99,6 +106,7 @@
             pl.semaphore_signal(barrier, inc=1, device_id={"lon": lax.rem(d + j, NLONDEV)}, device_id_type=MESH)
             return carry
 
+        tell_lat(barrier)
         lax.fori_loop(1, NLONDEV, greet, 0)
 
     loads[0].wait()
@@ -109,7 +117,8 @@
             send1[s, pl.ds(hi, OWNERS, stride=2), :] = packed[at:at + OWNERS]
 
     one = owner.astype(jnp.int32)
-    pl.semaphore_wait(barrier, OWNERS - one + 3 * (north.astype(jnp.int32) + south.astype(jnp.int32)))
+    sides = north.astype(jnp.int32) + south.astype(jnp.int32)
+    pl.semaphore_wait(barrier, OWNERS - one + one * sides)
     mine, ranked = pl.ds(2 * d, 2), pl.ds(2 * rank, 2)
 
     def collect(j, carry):
@@ -130,12 +139,14 @@
     def _():
         pltpu.make_async_copy(send1.at[:, ranked], recv1.at[:, mine], sems.at[1]).start()
         pltpu.make_async_copy(recv1, recv1, sems.at[1]).wait()
+        tell_lat(lat_in)
         for s in range(REP):
-            work[s] = recv1[s].T
+            own = [rank + OWNERS * s + 64 * c for c in range(4)]
+            turns = [offsets[i] for i in own]
+            work[s] = shift_coarse(recv1[s], by_chunk(lane_iota(8) // 32, turns, jnp.int32)).T
             v = [work[s, pl.ds(r, 8, stride=16), :] for r in range(16)]
-            own = [rank + OWNERS * s + 64 * c for c in range(4)]
-            v = shift_rows(v, by_chunk([offsets[i] for i in own], jnp.int32))
-            v = interpolate(v, by_chunk([fraction[i] for i in own], jnp.float32))
+            v = shift_fine(v, by_chunk(sub_iota() // 2, turns, jnp.int32))
+            v = interpolate(v, by_chunk(sub_iota() // 2, [fraction[i] for i in own], jnp.float32))
             for r in range(16):
                 work[s, pl.ds(r, 8, stride=16), :] = v[r]
             send2[s] = work[s].T
@@ -156,6 +167,9 @@
 
         lax.fori_loop(0, NLONDEV, spread, 0)
         pltpu.make_async_copy(send2.at[:, mine], recv2.at[:, ranked], sems.at[3]).start()
+        pl.semaphore_wait(lat_in, sides)
+        for i in range(OWNERS, NLONDEV, OWNERS):
+            pl.semaphore_signal(may_near, inc=1, device_id={"lon": lax.rem(d + i, NLONDEV)}, device_id_type=MESH)
 
     pltpu.make_async_copy(recv2, recv2, sems.at[3]).wait()
     ext[1, 32:160, :] = jnp.concatenate(
@@ -176,6 +190,11 @@
 
     for dd in (-1, 1):
         near(dd, 0).start()
+
+    @pl.when(jnp.logical_not(owner))
+    def _():
+        pl.semaphore_wait(may_near, 1)
+
     for there, to in ((north, -1), (south, 1)):
         @pl.when(there)
         def _():
@@ -337,6 +356,8 @@
             pltpu.SemaphoreType.DMA((4,)),
             pltpu.SemaphoreType.DMA((3, 3)),
             pltpu.SemaphoreType.DMA((3, 3)),
+            pltpu.SemaphoreType.REGULAR,
+            pltpu.SemaphoreType.REGULAR,
         ],
         compiler_params=pltpu.CompilerParams(collective_id=0, has_side_effects=True, vmem_limit_bytes=16 * 1024 * 1024),
     )(*(pltpu.with_memory_space_constraint(a, pltpu.HBM) for a in (field, offsets, fraction)))

time: 42.6 us -> 41.2 us (0.967)
  Pallas kernels: 42.4 us -> 41 us
    pallas_call x1, Pallas kernels: 39.7 us -> 38.3 us  [per_device(): pl.pallas_call(exchange_kernel, out_shape=jax.ShapeDtypeStruct((3, 192, L...]
where the time goes in v5:
time: 41.2 us; the launch traced here: 41.1 us
  Pallas kernels  41 us (100%)
    pallas_call x1, Pallas kernels, per_device(): pl.pallas_call(exchange_kernel, out_shape=jax.ShapeDtypeStruct((3, 192, L...  38.3 us
    pallas_call x1, Pallas kernels, per_device(): pl.pallas_call(cycle_kernel, out_shape=jax.ShapeDtypeStruct(field.shape,...  2.7 us

profile of v5, /device:TPU:6, one launch (start us, length us, event | category | flops | bytes accessed | tf_op | source)
XLA Modules:
  0.0 41.1 jit_solution(10722235790498123273)
XLA Ops:
  0.0 0.0 copy-start
  0.0 38.3 %shard_map.46.ext = f32[3,192,128]{2,1,0:T(8,128)S(1)} custom-call(f32[2,32,256]{2,1,0:T(8,128)} %field_in.1, s32[256]{0:T(256)} %offsets_in.1, f32[256]{0:T(256)} %fraction_in.1), custom_call_target="tpu_custom_call" | custom-call | tf_op jit(solution)/shard_map/pallas_call | solution.py:345
  38.3 0.0 copy-done
  38.3 2.7 %shard_map.47 = f32[2,32,256]{2,1,0:T(8,128)} custom-call(f32[3,192,128]{2,1,0:T(8,128)S(1)} %shard_map.46.ext, f32[2]{0:T(128)S(1)} %copy-done), custom_call_target="tpu_custom_call" | custom-call | tf_op jit(solution)/shard_map/pallas_call | solution.py:364
Async XLA Ops:
  0.0 38.3 %copy-start = (f32[2]{0:T(128)S(1)}, f32[2]{0:T(128)}, u32[]{:S(2)}) copy-start(f32[2]{0:T(128)} %helm.1) | copy-start | bytes 28

commit v6 on v5

--- a/solution.py
+++ b/solution.py
@@ -80,7 +80,8 @@
 
 
 def exchange_kernel(field_in, offsets_in, fraction_in, ext, field, offsets, fraction, send1, recv1, send2, recv2, work,
-                    load_sems, sems, near_send, near_recv, lat_in, may_near):
+                    beside,
+                    load_sems, sems, beside_send, beside_recv, near_send, near_recv, lat_in, may_near):
     d = lax.axis_index("lon")
     g = lax.axis_index("lat")
     north, south = g > 0, g < NLATDEV - 1
@@ -152,44 +153,55 @@
             send2[s] = work[s].T
 
         def spread(j, carry):
-            k = j // 4 - PLANES
-            plane = jnp.where(k < 0, k + PLANES, jnp.where(k % 2 == 0, 15 - k // 2, PLANES + k // 2))
+            k = j // 4
+            far = k - PLANES - 1
+            plane = jnp.where(far % 2 == 0, PLANES + far // 2, 10 + far // 2)
+            plane = jnp.where(k == 0, 15, jnp.where(far < 0, k - 1, plane))
             to = lax.rem(4 * (plane + FIRST) + lax.rem(j + d, 4), NLONDEV)
 
             @pl.when(to != d)
             def _():
                 pltpu.make_async_remote_copy(
                     src_ref=send2.at[:, pl.ds(2 * to, 2)], dst_ref=recv2.at[:, ranked],
-                    send_sem=sems.at[2], recv_sem=sems.at[3],
+                    send_sem=sems.at[2], recv_sem=sems.at[3 + rank // 4],
                     device_id={"lon": to}, device_id_type=MESH,
                 ).start()
             return carry
 
         lax.fori_loop(0, NLONDEV, spread, 0)
-        pltpu.make_async_copy(send2.at[:, mine], recv2.at[:, ranked], sems.at[3]).start()
+        pltpu.make_async_copy(send2.at[:, mine], recv2.at[:, ranked], sems.at[3 + rank // 4]).start()
         pl.semaphore_wait(lat_in, sides)
         for i in range(OWNERS, NLONDEV, OWNERS):
             pl.semaphore_signal(may_near, inc=1, device_id={"lon": lax.rem(d + i, NLONDEV)}, device_id_type=MESH)
 
-    pltpu.make_async_copy(recv2, recv2, sems.at[3]).wait()
-    ext[1, 32:160, :] = jnp.concatenate(
-        [recv2[s, pl.ds(hi, OWNERS, stride=2), :] for hi in range(2) for s in range(REP)], axis=0).T
+    falling = (rank >= OWNERS) & (rank < 40)
+    for k in range(PLANES):
+        p = jnp.where(falling, PLANES - 1 - k, k)
+        part = recv2.at[:, pl.ds(pl.multiple_of(8 * p, 8), 8)]
+        pltpu.make_async_copy(part, part, sems.at[3 + p]).wait()
+        for side, dd in ((0, 1), (1, -1)):
+            pltpu.make_async_remote_copy(
+                src_ref=part, dst_ref=beside.at[side, :, pl.ds(pl.multiple_of(8 * p, 8), 8)],
+                send_sem=beside_send.at[side], recv_sem=beside_recv.at[side],
+                device_id={"lon": lax.rem(d + dd + NLONDEV, NLONDEV)}, device_id_type=MESH,
+            ).start()
+
+    def turned(rows):
+        return jnp.concatenate(
+            [rows[s, pl.ds(hi, OWNERS, stride=2), :] for hi in range(2) for s in range(REP)], axis=0).T
+
+    ext[1, 32:160, :] = turned(recv2)
 
     def near(dd, to):
-        if to == 0:
-            src, dst = ext.at[1, pl.ds(32, 128)], ext.at[1 - dd, pl.ds(32, 128)]
-        elif to < 0:
+        if to < 0:
             src, dst = ext.at[1, pl.ds(32, 32)], ext.at[1 - dd, pl.ds(160, 32)]
         else:
             src, dst = ext.at[1, pl.ds(128, 32)], ext.at[1 - dd, pl.ds(0, 32)]
         return pltpu.make_async_remote_copy(
             src_ref=src, dst_ref=dst,
-            send_sem=near_send.at[to + 1, dd + 1], recv_sem=near_recv.at[to + 1, dd + 1],
+            send_sem=near_send.at[(to + 1) // 2, dd + 1], recv_sem=near_recv.at[(to + 1) // 2, dd + 1],
             device_id={"lon": lax.rem(d + dd + NLONDEV, NLONDEV), "lat": g + to},
             device_id_type=MESH)
-
-    for dd in (-1, 1):
-        near(dd, 0).start()
 
     @pl.when(jnp.logical_not(owner))
     def _():
@@ -206,24 +218,26 @@
             for k in range(3):
                 ext[k, at:at + 32, :] = jnp.zeros((32, LANES), jnp.float32)
 
-    @pl.when(owner)
-    def _():
-        for src, i in ((send1, 0), (send2, 2)):
-            part = src.at[:, pl.ds(0, src.shape[1] - 2)]
-            pltpu.make_async_copy(part, part, sems.at[i]).wait()
-
-    @pl.when(jnp.logical_not(owner))
-    def _():
-        pltpu.make_async_copy(send1, send1, sems.at[0]).wait()
-
-    for dd in (-1, 1):
-        near(dd, 0).wait()
+    for side in range(2):
+        pltpu.make_async_copy(beside.at[side], beside.at[side], beside_recv.at[side]).wait()
+        ext[2 * side, 32:160, :] = turned(beside.at[side])
+        pltpu.make_async_copy(recv2, recv2, beside_send.at[side]).wait()
     for there, to in ((north, -1), (south, 1)):
         @pl.when(there)
         def _():
             for dd in (-1, 0, 1):
                 near(dd, to).wait_send()
                 near(dd, -to).wait_recv()
+
+    @pl.when(owner)
+    def _():
+        for src, i in ((send1, 0), (send2, 2)):
+            part = src.at[:, pl.ds(0, src.shape[1] - 2)]
+            pltpu.make_async_copy(part, part, sems.at[i]).wait()
+
+    @pl.when(jnp.logical_not(owner))
+    def _():
+        pltpu.make_async_copy(send1, send1, sems.at[0]).wait()
 
 
 def memo(f):
@@ -352,10 +366,13 @@
             pltpu.SMEM(offsets.shape, jnp.int32),
             pltpu.SMEM(fraction.shape, jnp.float32),
             parts, circles, circles, parts, circles,
+            pltpu.VMEM((2, REP, 2 * OWNERS, LANES), jnp.float32),
             pltpu.SemaphoreType.DMA((3,)),
-            pltpu.SemaphoreType.DMA((4,)),
-            pltpu.SemaphoreType.DMA((3, 3)),
-            pltpu.SemaphoreType.DMA((3, 3)),
+            pltpu.SemaphoreType.DMA((3 + PLANES,)),
+            pltpu.SemaphoreType.DMA((2,)),
+            pltpu.SemaphoreType.DMA((2,)),
+            pltpu.SemaphoreType.DMA((2, 3)),
+            pltpu.SemaphoreType.DMA((2, 3)),
             pltpu.SemaphoreType.REGULAR,
             pltpu.SemaphoreType.REGULAR,
         ],

time: 41.2 us -> 40.5 us (0.983)
  the two profiles are of different devices: /device:TPU:6 before, /device:TPU:289 now
where the time goes in v6:
time: 40.5 us; the launch traced here: 40.3 us
  Pallas kernels  40.3 us (100%)
    pallas_call x1, Pallas kernels, per_device(): pl.pallas_call(exchange_kernel, out_shape=jax.ShapeDtypeStruct((3, 192, L...  37.6 us
    pallas_call x1, Pallas kernels, per_device(): pl.pallas_call(cycle_kernel, out_shape=jax.ShapeDtypeStruct(field.shape,...  2.7 us

profile of v6, /device:TPU:289, one launch (start us, length us, event | category | flops | bytes accessed | tf_op | source)
XLA Modules:
  0.0 40.3 jit_solution(3978920838604098013)
XLA Ops:
  0.0 0.0 copy-start
  0.0 37.6 %shard_map.46.ext = f32[3,192,128]{2,1,0:T(8,128)S(1)} custom-call(f32[2,32,256]{2,1,0:T(8,128)} %field_in.1, s32[256]{0:T(256)} %offsets_in.1, f32[256]{0:T(256)} %fraction_in.1), custom_call_target="tpu_custom_call" | custom-call | tf_op jit(solution)/shard_map/pallas_call | solution.py:359
  37.6 0.0 copy-done
  37.6 2.7 %shard_map.47 = f32[2,32,256]{2,1,0:T(8,128)} custom-call(f32[3,192,128]{2,1,0:T(8,128)S(1)} %shard_map.46.ext, f32[2]{0:T(128)S(1)} %copy-done), custom_call_target="tpu_custom_call" | custom-call | tf_op jit(solution)/shard_map/pallas_call | solution.py:381
Async XLA Ops:
  0.0 37.6 %copy-start = (f32[2]{0:T(128)S(1)}, f32[2]{0:T(128)}, u32[]{:S(2)}) copy-start(f32[2]{0:T(128)} %helm.1) | copy-start | bytes 28

commit v7 on v6

--- a/solution.py
+++ b/solution.py
@@ -12,6 +12,7 @@
 PLANES = 4
 OWNERS = 4 * PLANES
 REP = NLONDEV // OWNERS
+SPLIT = PLANES + (16 - PLANES) // 2
 LANES = 128
 
 
@@ -79,7 +80,7 @@
     return [w_one * ext[r + 3] + w_two * ext[r + 2] + w_three * ext[r + 1] + w_four * ext[r] for r in range(16)]
 
 
-def exchange_kernel(field_in, offsets_in, fraction_in, ext, field, offsets, fraction, send1, recv1, send2, recv2, work,
+def exchange_kernel(field_in, offsets_in, fraction_in, helm_in, ext, coef, field, offsets, fraction, helm, send1, recv1, send2, recv2, work,
                     beside,
                     load_sems, sems, beside_send, beside_recv, near_send, near_recv, lat_in, may_near):
     d = lax.axis_index("lon")
@@ -89,7 +90,7 @@
     owner = rank < OWNERS
 
     loads = [pltpu.make_async_copy(src, dst, load_sems.at[i]) for i, (src, dst) in enumerate(
-        ((field_in, field), (offsets_in, offsets), (fraction_in, fraction)))]
+        ((field_in, field), (offsets_in, offsets), (fraction_in, fraction), (helm_in, helm)))]
     for load in loads:
         load.start()
 
@@ -104,11 +105,15 @@
     @pl.when(owner)
     def _():
         def greet(j, carry):
-            pl.semaphore_signal(barrier, inc=1, device_id={"lon": lax.rem(d + j, NLONDEV)}, device_id_type=MESH)
+            to = lax.rem(OWNERS + 4 * FIRST + j, NLONDEV)
+
+            @pl.when(to != d)
+            def _():
+                pl.semaphore_signal(barrier, inc=1, device_id={"lon": to}, device_id_type=MESH)
             return carry
 
         tell_lat(barrier)
-        lax.fori_loop(1, NLONDEV, greet, 0)
+        lax.fori_loop(0, NLONDEV, greet, 0)
 
     loads[0].wait()
     packed = pack_field(lambda lev, hi, pair: field[lev, 16 * hi:16 * hi + 16, 128 * pair:128 * pair + 128]).T
@@ -133,8 +138,10 @@
         return carry
 
     lax.fori_loop(one, OWNERS, collect, 0)
-    loads[1].wait()
-    loads[2].wait()
+    for load in loads[1:]:
+        load.wait()
+    coef[...] = jnp.where(sub_iota() % 2 == 0, jnp.full((8, LANES), helm[0], jnp.float32),
+                          jnp.full((8, LANES), helm[1], jnp.float32))
 
     @pl.when(owner)
     def _():
@@ -155,7 +162,7 @@
         def spread(j, carry):
             k = j // 4
             far = k - PLANES - 1
-            plane = jnp.where(far % 2 == 0, PLANES + far // 2, 10 + far // 2)
+            plane = jnp.where(far % 2 == 0, PLANES + far // 2, SPLIT + far // 2)
             plane = jnp.where(k == 0, 15, jnp.where(far < 0, k - 1, plane))
             to = lax.rem(4 * (plane + FIRST) + lax.rem(j + d, 4), NLONDEV)
 
@@ -174,7 +181,7 @@
         for i in range(OWNERS, NLONDEV, OWNERS):
             pl.semaphore_signal(may_near, inc=1, device_id={"lon": lax.rem(d + i, NLONDEV)}, device_id_type=MESH)
 
-    falling = (rank >= OWNERS) & (rank < 40)
+    falling = (rank >= OWNERS) & (rank < 4 * SPLIT)
     for k in range(PLANES):
         p = jnp.where(falling, PLANES - 1 - k, k)
         part = recv2.at[:, pl.ds(pl.multiple_of(8 * p, 8), 8)]
@@ -333,41 +340,46 @@
     return jnp.where(out, 0.0, 1.0)
 
 
-def cycle_kernel(ext, helm, out, rows):
+def cycle_kernel(ext, coef, out, rows, block, sems):
     g = lax.axis_index("lat")
-    lev = sub_iota() % 2
-    c0 = jnp.where(lev == 0, jnp.full((8, LANES), helm[0], jnp.float32), jnp.full((8, LANES), helm[1], jnp.float32))
-    result = v_cycle(window(lambda k, at: ext[k, pl.ds(at, 8, stride=16), :]), c0, inside_of(g))
-    for i in range(32):
-        rows[8 * i:8 * i + 8, :] = result(i)
+    result = v_cycle(window(lambda k, at: ext[k, pl.ds(at, 8, stride=16), :]), coef[...], inside_of(g))
     low = lane_iota(8) < 64
-    for block in range(4):
+    copies = []
+    for b in range(4):
+        for i in range(8 * b, 8 * b + 8):
+            rows[8 * i:8 * i + 8, :] = result(i)
         for lev in range(2):
             for pair in range(2):
-                left = rows[pl.ds(64 * block + 4 * pair + lev, 8, stride=8), :]
-                right = rows[pl.ds(64 * block + 4 * pair + 2 + lev, 8, stride=8), :]
-                out[lev, 8 * block:8 * block + 8, 128 * pair:128 * pair + 128] = jnp.where(
+                left = rows[pl.ds(64 * b + 4 * pair + lev, 8, stride=8), :]
+                right = rows[pl.ds(64 * b + 4 * pair + 2 + lev, 8, stride=8), :]
+                block[lev, 8 * b:8 * b + 8, 128 * pair:128 * pair + 128] = jnp.where(
                     low, roll(left, -32), roll(right, 32))
+        part = (slice(None), pl.ds(8 * b, 8))
+        copies.append(pltpu.make_async_copy(block.at[part], out.at[part], sems.at[b]))
+        copies[-1].start()
+    for copy in copies:
+        copy.wait()
 
 
 def per_device(field, offsets, fraction, helm):
     vmem = pl.BlockSpec(memory_space=pltpu.VMEM)
-    smem = pl.BlockSpec(memory_space=pltpu.SMEM)
     hbm = pl.BlockSpec(memory_space=pltpu.HBM)
     parts = pltpu.VMEM((REP, 2 * OWNERS, LANES), jnp.float32)
     circles = pltpu.VMEM((REP, LANES, LANES), jnp.float32)
-    ext = pl.pallas_call(
+    inputs = [pltpu.with_memory_space_constraint(a, pltpu.HBM) for a in (field, offsets, fraction, helm)]
+    ext, coef = pl.pallas_call(
         exchange_kernel,
-        out_shape=jax.ShapeDtypeStruct((3, 192, LANES), jnp.float32),
-        in_specs=[hbm, hbm, hbm],
-        out_specs=vmem,
+        out_shape=(jax.ShapeDtypeStruct((3, 192, LANES), jnp.float32), jax.ShapeDtypeStruct((8, LANES), jnp.float32)),
+        in_specs=[hbm] * 4,
+        out_specs=(vmem, vmem),
         scratch_shapes=[
             pltpu.VMEM(field.shape, jnp.float32),
             pltpu.SMEM(offsets.shape, jnp.int32),
             pltpu.SMEM(fraction.shape, jnp.float32),
+            pltpu.SMEM(helm.shape, jnp.float32),
             parts, circles, circles, parts, circles,
             pltpu.VMEM((2, REP, 2 * OWNERS, LANES), jnp.float32),
-            pltpu.SemaphoreType.DMA((3,)),
+            pltpu.SemaphoreType.DMA((4,)),
             pltpu.SemaphoreType.DMA((3 + PLANES,)),
             pltpu.SemaphoreType.DMA((2,)),
             pltpu.SemaphoreType.DMA((2,)),
@@ -377,15 +389,19 @@
             pltpu.SemaphoreType.REGULAR,
         ],
         compiler_params=pltpu.CompilerParams(collective_id=0, has_side_effects=True, vmem_limit_bytes=16 * 1024 * 1024),
-    )(*(pltpu.with_memory_space_constraint(a, pltpu.HBM) for a in (field, offsets, fraction)))
+    )(*inputs)
     return pl.pallas_call(
         cycle_kernel,
         out_shape=jax.ShapeDtypeStruct(field.shape, jnp.float32),
-        in_specs=[vmem, smem],
-        out_specs=vmem,
-        scratch_shapes=[pltpu.VMEM((256, LANES), jnp.float32)],
+        in_specs=[vmem, vmem],
+        out_specs=hbm,
+        scratch_shapes=[
+            pltpu.VMEM((256, LANES), jnp.float32),
+            pltpu.VMEM(field.shape, jnp.float32),
+            pltpu.SemaphoreType.DMA((4,)),
+        ],
         compiler_params=pltpu.CompilerParams(vmem_limit_bytes=16 * 1024 * 1024),
-    )(ext, helm)
+    )(ext, coef)
 
 
 def solution(mesh):

time: 40.5 us -> 39.7 us (0.980)
  Pallas kernels: 40.3 us -> 39.6 us
    pallas_call x1, Pallas kernels: 2.7 us -> 2.25 us  [per_device(): pl.pallas_call(cycle_kernel, out_shape=jax.ShapeDtypeStruct(field.shape,...]
where the time goes in v7:
time: 39.7 us; the launch traced here: 39.6 us
  Pallas kernels  39.6 us (100%)
    pallas_call x1, Pallas kernels, per_device(): pl.pallas_call(exchange_kernel, out_shape=(jax.ShapeDtypeStruct((3, 192,...  37.4 us
    pallas_call x1, Pallas kernels, per_device(): pl.pallas_call(cycle_kernel, out_shape=jax.ShapeDtypeStruct(field.shape,...  2.25 us

profile of v7, /device:TPU:289, one launch (start us, length us, event | category | flops | bytes accessed | tf_op | source)
XLA Modules:
  0.0 39.6 jit_solution(11308062006296372685)
XLA Ops:
  0.0 37.4 %shard_map.46 = (f32[3,192,128]{2,1,0:T(8,128)S(1)}, f32[8,128]{1,0:T(8,128)S(1)}) custom-call(f32[2,32,256]{2,1,0:T(8,128)} %field_in.1, s32[256]{0:T(256)} %offsets_in.1, f32[256]{0:T(256)} %fraction_in.1, f32[2]{0:T(128)} %helm_in.1), custom_call_target="tpu_custom_call" | custom-call | tf_op jit(solution)/shard_map/pallas_call | solution.py:370
  37.4 2.3 %shard_map.47 = f32[2,32,256]{2,1,0:T(8,128)} custom-call(f32[3,192,128]{2,1,0:T(8,128)S(1)} %get-tuple-element.7.ext, f32[8,128]{1,0:T(8,128)S(1)} %get-tuple-element.8.coef), custom_call_target="tpu_custom_call" | custom-call | tf_op jit(solution)/shard_map/pallas_call | solution.py:393

commit v8 on v7

--- a/solution.py
+++ b/solution.py
@@ -12,6 +12,7 @@
 PLANES = 4
 OWNERS = 4 * PLANES
 REP = NLONDEV // OWNERS
+SERVED = (15, 4, 0, 5, 1, 6, 2, 7, 3, 8, 9, 10, 11, 12, 13, 14)
 SPLIT = PLANES + (16 - PLANES) // 2
 LANES = 128
 
@@ -89,8 +90,10 @@
     rank = lax.rem(d + NLONDEV - 4 * FIRST, NLONDEV)
     owner = rank < OWNERS
 
+    parts = [(lev, pl.ds(16 * hi, 16)) for lev in range(2) for hi in range(2)]
     loads = [pltpu.make_async_copy(src, dst, load_sems.at[i]) for i, (src, dst) in enumerate(
-        ((field_in, field), (offsets_in, offsets), (fraction_in, fraction), (helm_in, helm)))]
+        [(field_in.at[at], field.at[at]) for at in parts]
+        + [(offsets_in, offsets), (fraction_in, fraction), (helm_in, helm)])]
     for load in loads:
         load.start()
 
@@ -115,7 +118,8 @@
         tell_lat(barrier)
         lax.fori_loop(0, NLONDEV, greet, 0)
 
-    loads[0].wait()
+    for load in loads[:4]:
+        load.wait()
     packed = pack_field(lambda lev, hi, pair: field[lev, 16 * hi:16 * hi + 16, 128 * pair:128 * pair + 128]).T
     for hi in range(2):
         for s in range(REP):
@@ -128,7 +132,9 @@
     mine, ranked = pl.ds(2 * d, 2), pl.ds(2 * rank, 2)
 
     def collect(j, carry):
-        to_rank = lax.rem(rank + j, OWNERS)
+        k = j // 4
+        farthest = 4 * jnp.where(d >= 40, PLANES - 1 - k, k) + lax.rem(j + d, 4)
+        to_rank = jnp.where(owner, lax.rem(rank + j, OWNERS), farthest)
         to = lax.rem(to_rank + 4 * FIRST, NLONDEV)
         pltpu.make_async_remote_copy(
             src_ref=send1.at[:, pl.ds(2 * to_rank, 2)], dst_ref=recv1.at[:, mine],
@@ -138,7 +144,7 @@
         return carry
 
     lax.fori_loop(one, OWNERS, collect, 0)
-    for load in loads[1:]:
+    for load in loads[4:]:
         load.wait()
     coef[...] = jnp.where(sub_iota() % 2 == 0, jnp.full((8, LANES), helm[0], jnp.float32),
                           jnp.full((8, LANES), helm[1], jnp.float32))
@@ -159,23 +165,21 @@
                 work[s, pl.ds(r, 8, stride=16), :] = v[r]
             send2[s] = work[s].T
 
-        def spread(j, carry):
-            k = j // 4
-            far = k - PLANES - 1
-            plane = jnp.where(far % 2 == 0, PLANES + far // 2, SPLIT + far // 2)
-            plane = jnp.where(k == 0, 15, jnp.where(far < 0, k - 1, plane))
-            to = lax.rem(4 * (plane + FIRST) + lax.rem(j + d, 4), NLONDEV)
-
-            @pl.when(to != d)
-            def _():
-                pltpu.make_async_remote_copy(
-                    src_ref=send2.at[:, pl.ds(2 * to, 2)], dst_ref=recv2.at[:, ranked],
-                    send_sem=sems.at[2], recv_sem=sems.at[3 + rank // 4],
-                    device_id={"lon": to}, device_id_type=MESH,
-                ).start()
-            return carry
-
-        lax.fori_loop(0, NLONDEV, spread, 0)
+        for plane in SERVED:
+            def spread(j, carry):
+                to = 4 * plane + lax.rem(j + d, 4)
+
+                @pl.when(to != d)
+                def _():
+                    pltpu.make_async_remote_copy(
+                        src_ref=send2.at[:, pl.ds(2 * to, 2)], dst_ref=recv2.at[:, ranked],
+                        send_sem=sems.at[2], recv_sem=sems.at[3 + rank // 4],
+                        device_id={"lon": to}, device_id_type=MESH,
+                    ).start()
+                return carry
+
+            lax.fori_loop(0, 4, spread, 0)
+
         pltpu.make_async_copy(send2.at[:, mine], recv2.at[:, ranked], sems.at[3 + rank // 4]).start()
         pl.semaphore_wait(lat_in, sides)
         for i in range(OWNERS, NLONDEV, OWNERS):
@@ -379,7 +383,7 @@
             pltpu.SMEM(helm.shape, jnp.float32),
             parts, circles, circles, parts, circles,
             pltpu.VMEM((2, REP, 2 * OWNERS, LANES), jnp.float32),
-            pltpu.SemaphoreType.DMA((4,)),
+            pltpu.SemaphoreType.DMA((7,)),
             pltpu.SemaphoreType.DMA((3 + PLANES,)),
             pltpu.SemaphoreType.DMA((2,)),
             pltpu.SemaphoreType.DMA((2,)),

time: 39.7 us -> 38.5 us (0.970)
  the two profiles are of different devices: /device:TPU:289 before, /device:TPU:291 now
where the time goes in v8:
time: 38.5 us; the launch traced here: 38.3 us
  Pallas kernels  38.3 us (99%)
    pallas_call x1, Pallas kernels, per_device(): pl.pallas_call(exchange_kernel, out_shape=(jax.ShapeDtypeStruct((3, 192,...  36 us
    pallas_call x1, Pallas kernels, per_device(): pl.pallas_call(cycle_kernel, out_shape=jax.ShapeDtypeStruct(field.shape,...  2.25 us

profile of v8, /device:TPU:291, one launch (start us, length us, event | category | flops | bytes accessed | tf_op | source)
XLA Modules:
  0.0 38.3 jit_solution(611970450177282804)
XLA Ops:
  0.0 36.0 %shard_map.46 = (f32[3,192,128]{2,1,0:T(8,128)S(1)}, f32[8,128]{1,0:T(8,128)S(1)}) custom-call(f32[2,32,256]{2,1,0:T(8,128)} %field_in.1, s32[256]{0:T(256)} %offsets_in.1, f32[256]{0:T(256)} %fraction_in.1, f32[2]{0:T(128)} %helm_in.1), custom_call_target="tpu_custom_call" | custom-call | tf_op jit(solution)/shard_map/pallas_call | solution.py:374
  36.0 2.3 %shard_map.47 = f32[2,32,256]{2,1,0:T(8,128)} custom-call(f32[3,192,128]{2,1,0:T(8,128)S(1)} %get-tuple-element.7.ext, f32[8,128]{1,0:T(8,128)S(1)} %get-tuple-element.8.coef), custom_call_target="tpu_custom_call" | custom-call | tf_op jit(solution)/shard_map/pallas_call | solution.py:397

commit v9 on v8

--- a/solution.py
+++ b/solution.py
@@ -12,7 +12,7 @@
 PLANES = 4
 OWNERS = 4 * PLANES
 REP = NLONDEV // OWNERS
-SERVED = (15, 4, 0, 5, 1, 6, 2, 7, 3, 8, 9, 10, 11, 12, 13, 14)
+SERVED = (15, 4, 0, 5, 1, 6, 2, 9, 3, 7, 8, 10, 11, 12, 13, 14)
 SPLIT = PLANES + (16 - PLANES) // 2
 LANES = 128
 
@@ -330,17 +330,15 @@
         k, hi, r = (i + 32) // 32, (i % 32) // 16, i % 16
         before, here, after = rows(k, r), rows(k, r + 32), rows(k, r + 64)
         if hi == 0:
-            sides = roll(jnp.where(lane < 32, after, before), -32)
-            return jnp.where((lane >= 32) & (lane < 96), roll(here, 32), sides)
-        sides = roll(jnp.where(lane < 96, after, before), 32)
-        return jnp.where((lane >= 32) & (lane < 96), roll(here, -32), sides)
+            return jnp.where(lane < 64, here, roll(jnp.where(lane < 32, after, before), 64))
+        return jnp.where(lane < 64, roll(here, 64), jnp.where(lane < 96, after, before))
 
     return load
 
 
 def inside_of(g):
     chunk, lane = sub_iota() // 2, lane_iota(8)
-    out = ((g == 0) & (chunk == 0) & (lane < 32)) | ((g == NLATDEV - 1) & (chunk == 3) & (lane >= 96))
+    out = ((g == 0) & (chunk == 0) & (lane >= 96)) | ((g == NLATDEV - 1) & (chunk == 3) & (lane >= 64) & (lane < 96))
     return jnp.where(out, 0.0, 1.0)
 
 
@@ -357,7 +355,7 @@
                 left = rows[pl.ds(64 * b + 4 * pair + lev, 8, stride=8), :]
                 right = rows[pl.ds(64 * b + 4 * pair + 2 + lev, 8, stride=8), :]
                 block[lev, 8 * b:8 * b + 8, 128 * pair:128 * pair + 128] = jnp.where(
-                    low, roll(left, -32), roll(right, 32))
+                    low, left, roll(right, 64))
         part = (slice(None), pl.ds(8 * b, 8))
         copies.append(pltpu.make_async_copy(block.at[part], out.at[part], sems.at[b]))
         copies[-1].start()

time: 38.5 us -> 38.3 us (level)
  the two profiles are of different devices: /device:TPU:291 before, /device:TPU:293 now
where the time goes in v9:
time: 38.3 us; the launch traced here: 38.1 us
  Pallas kernels  38.1 us (99%)
    pallas_call x1, Pallas kernels, per_device(): pl.pallas_call(exchange_kernel, out_shape=(jax.ShapeDtypeStruct((3, 192,...  35.9 us
    pallas_call x1, Pallas kernels, per_device(): pl.pallas_call(cycle_kernel, out_shape=jax.ShapeDtypeStruct(field.shape,...  2.17 us

profile of v9, /device:TPU:293, one launch (start us, length us, event | category | flops | bytes accessed | tf_op | source)
XLA Modules:
  0.0 38.1 jit_solution(381715663672463306)
XLA Ops:
  0.0 35.9 %shard_map.46 = (f32[3,192,128]{2,1,0:T(8,128)S(1)}, f32[8,128]{1,0:T(8,128)S(1)}) custom-call(f32[2,32,256]{2,1,0:T(8,128)} %field_in.1, s32[256]{0:T(256)} %offsets_in.1, f32[256]{0:T(256)} %fraction_in.1, f32[2]{0:T(128)} %helm_in.1), custom_call_target="tpu_custom_call" | custom-call | tf_op jit(solution)/shard_map/pallas_call | solution.py:372
  35.9 2.2 %shard_map.47 = f32[2,32,256]{2,1,0:T(8,128)} custom-call(f32[3,192,128]{2,1,0:T(8,128)S(1)} %get-tuple-element.7.ext, f32[8,128]{1,0:T(8,128)S(1)} %get-tuple-element.8.coef), custom_call_target="tpu_custom_call" | custom-call | tf_op jit(solution)/shard_map/pallas_call | solution.py:395

commit v10 on v9

--- a/solution.py
+++ b/solution.py
@@ -292,12 +292,14 @@
         return memo(lambda i: (rhs(i) - diag * x(i)) + mult * s(i))
 
     def restrict(x, step):
-        even = (lane // step) % 2 == 0
-
         def f(i):
             q = x(2 * i) + x(2 * i + 1)
-            return 0.25 * (q + jnp.where(even, roll(q, -step), roll(q, step)))
+            return 0.25 * (q + roll(q, -step))
         return memo(f)
+
+    def filled(x, step):
+        first = (lane // step) % 2 == 0
+        return memo(lambda i: jnp.where(first, x(i), roll(x(i), step)))
 
     def all_of(f, low, high):
         for i in range(low, high + 1):
@@ -315,10 +317,12 @@
     x2 = all_of(second(first2, gamma2, 4), -4, 11)
     x2 = all_of(sweep(x2, first2, gamma2, 4), -3, 10)
     x2 = all_of(sweep(x2, first2, gamma2, 4), -2, 9)
-    y1 = all_of(memo(lambda i: x1(i) + x2(i >> 1)), -3, 18)
+    fill2 = all_of(filled(x2, 2), -2, 9)
+    y1 = all_of(memo(lambda i: x1(i) + fill2(i >> 1)), -3, 18)
     y1 = all_of(sweep(y1, first1, gamma1, 2), -2, 17)
     y1 = all_of(sweep(y1, first1, gamma1, 2), -1, 16)
-    y0 = all_of(memo(lambda i: x0(i) + y1(i >> 1)), -2, 33)
+    fill1 = all_of(filled(y1, 1), -1, 16)
+    y0 = all_of(memo(lambda i: x0(i) + fill1(i >> 1)), -2, 33)
     y0 = all_of(sweep(y0, first0, gamma0, 1), -1, 32)
     return sweep(y0, first0, gamma0, 1)
 

time: 38.3 us -> 38.6 us (level)
  no operation moved by 1% of the time
where the time goes in v10:
time: 38.6 us; the launch traced here: 38.4 us
  Pallas kernels  38.4 us (99%)
    pallas_call x1, Pallas kernels, per_device(): pl.pallas_call(exchange_kernel, out_shape=(jax.ShapeDtypeStruct((3, 192,...  35.9 us
    pallas_call x1, Pallas kernels, per_device(): pl.pallas_call(cycle_kernel, out_shape=jax.ShapeDtypeStruct(field.shape,...  2.49 us

profile of v10, /device:TPU:293, one launch (start us, length us, event | category | flops | bytes accessed | tf_op | source)
XLA Modules:
  0.0 38.4 jit_solution(15624486591991977845)
XLA Ops:
  0.0 35.9 %shard_map.46 = (f32[3,192,128]{2,1,0:T(8,128)S(1)}, f32[8,128]{1,0:T(8,128)S(1)}) custom-call(f32[2,32,256]{2,1,0:T(8,128)} %field_in.1, s32[256]{0:T(256)} %offsets_in.1, f32[256]{0:T(256)} %fraction_in.1, f32[2]{0:T(128)} %helm_in.1), custom_call_target="tpu_custom_call" | custom-call | tf_op jit(solution)/shard_map/pallas_call | solution.py:376
  35.9 2.5 %shard_map.47 = f32[2,32,256]{2,1,0:T(8,128)} custom-call(f32[3,192,128]{2,1,0:T(8,128)S(1)} %get-tuple-element.7.ext, f32[8,128]{1,0:T(8,128)S(1)} %get-tuple-element.8.coef), custom_call_target="tpu_custom_call" | custom-call | tf_op jit(solution)/shard_map/pallas_call | solution.py:399

commit v11 on v9

--- a/solution.py
+++ b/solution.py
@@ -130,6 +130,10 @@
     sides = north.astype(jnp.int32) + south.astype(jnp.int32)
     pl.semaphore_wait(barrier, OWNERS - one + one * sides)
     mine, ranked = pl.ds(2 * d, 2), pl.ds(2 * rank, 2)
+
+    def block(ref, i):
+        return ref.at[pl.ds(pl.multiple_of(8 * i, 8), 8)]
+
 
     def collect(j, carry):
         k = j // 4
@@ -163,7 +167,9 @@
             v = interpolate(v, by_chunk(sub_iota() // 2, [fraction[i] for i in own], jnp.float32))
             for r in range(16):
                 work[s, pl.ds(r, 8, stride=16), :] = v[r]
-            send2[s] = work[s].T
+            work[s] = work[s].T
+            for hi in range(2):
+                send2[pl.ds(2 * s + hi, 64, stride=8), :] = work[s, pl.ds(hi, 64, stride=2), :]
 
         for plane in SERVED:
             def spread(j, carry):
@@ -172,7 +178,7 @@
                 @pl.when(to != d)
                 def _():
                     pltpu.make_async_remote_copy(
-                        src_ref=send2.at[:, pl.ds(2 * to, 2)], dst_ref=recv2.at[:, ranked],
+                        src_ref=block(send2, to), dst_ref=block(recv2, rank),
                         send_sem=sems.at[2], recv_sem=sems.at[3 + rank // 4],
                         device_id={"lon": to}, device_id_type=MESH,
                     ).start()
@@ -180,7 +186,7 @@
 
             lax.fori_loop(0, 4, spread, 0)
 
-        pltpu.make_async_copy(send2.at[:, mine], recv2.at[:, ranked], sems.at[3 + rank // 4]).start()
+        pltpu.make_async_copy(block(send2, d), block(recv2, rank), sems.at[3 + rank // 4]).start()
         pl.semaphore_wait(lat_in, sides)
         for i in range(OWNERS, NLONDEV, OWNERS):
             pl.semaphore_signal(may_near, inc=1, device_id={"lon": lax.rem(d + i, NLONDEV)}, device_id_type=MESH)
@@ -188,18 +194,19 @@
     falling = (rank >= OWNERS) & (rank < 4 * SPLIT)
     for k in range(PLANES):
         p = jnp.where(falling, PLANES - 1 - k, k)
-        part = recv2.at[:, pl.ds(pl.multiple_of(8 * p, 8), 8)]
+        rows = pl.ds(pl.multiple_of(32 * p, 32), 32)
+        part = recv2.at[rows]
         pltpu.make_async_copy(part, part, sems.at[3 + p]).wait()
         for side, dd in ((0, 1), (1, -1)):
             pltpu.make_async_remote_copy(
-                src_ref=part, dst_ref=beside.at[side, :, pl.ds(pl.multiple_of(8 * p, 8), 8)],
+                src_ref=part, dst_ref=beside.at[side, rows],
                 send_sem=beside_send.at[side], recv_sem=beside_recv.at[side],
                 device_id={"lon": lax.rem(d + dd + NLONDEV, NLONDEV)}, device_id_type=MESH,
             ).start()
 
     def turned(rows):
         return jnp.concatenate(
-            [rows[s, pl.ds(hi, OWNERS, stride=2), :] for hi in range(2) for s in range(REP)], axis=0).T
+            [rows[pl.ds(2 * s + hi, OWNERS, stride=8), :] for hi in range(2) for s in range(REP)], axis=0).T
 
     ext[1, 32:160, :] = turned(recv2)
 
@@ -242,8 +249,7 @@
 
     @pl.when(owner)
     def _():
-        for src, i in ((send1, 0), (send2, 2)):
-            part = src.at[:, pl.ds(0, src.shape[1] - 2)]
+        for part, i in ((send1.at[:, pl.ds(0, 2 * OWNERS - 2)], 0), (send2.at[pl.ds(0, 8 * NLONDEV - 8)], 2)):
             pltpu.make_async_copy(part, part, sems.at[i]).wait()
 
     @pl.when(jnp.logical_not(owner))
@@ -367,6 +373,7 @@
     vmem = pl.BlockSpec(memory_space=pltpu.VMEM)
     hbm = pl.BlockSpec(memory_space=pltpu.HBM)
     parts = pltpu.VMEM((REP, 2 * OWNERS, LANES), jnp.float32)
+    square = pltpu.VMEM((LANES, LANES), jnp.float32)
     circles = pltpu.VMEM((REP, LANES, LANES), jnp.float32)
     inputs = [pltpu.with_memory_space_constraint(a, pltpu.HBM) for a in (field, offsets, fraction, helm)]
     ext, coef = pl.pallas_call(
@@ -379,8 +386,8 @@
             pltpu.SMEM(offsets.shape, jnp.int32),
             pltpu.SMEM(fraction.shape, jnp.float32),
             pltpu.SMEM(helm.shape, jnp.float32),
-            parts, circles, circles, parts, circles,
-            pltpu.VMEM((2, REP, 2 * OWNERS, LANES), jnp.float32),
+            parts, circles, pltpu.VMEM((8 * NLONDEV, LANES), jnp.float32), square, circles,
+            pltpu.VMEM((2, LANES, LANES), jnp.float32),
             pltpu.SemaphoreType.DMA((7,)),
             pltpu.SemaphoreType.DMA((3 + PLANES,)),
             pltpu.SemaphoreType.DMA((2,)),

time: 38.3 us -> 38.5 us (level)
  the two profiles are of different devices: /device:TPU:293 before, /device:TPU:1 now
where the time goes in v11:
time: 38.5 us; the launch traced here: 38.4 us
  Pallas kernels  38.4 us (100%)
    pallas_call x1, Pallas kernels, per_device(): pl.pallas_call(exchange_kernel, out_shape=(jax.ShapeDtypeStruct((3, 192,...  36.2 us
    pallas_call x1, Pallas kernels, per_device(): pl.pallas_call(cycle_kernel, out_shape=jax.ShapeDtypeStruct(field.shape,...  2.17 us

profile of v11, /device:TPU:1, one launch (start us, length us, event | category | flops | bytes accessed | tf_op | source)
XLA Modules:
  0.0 38.4 jit_solution(3786622630380455977)
XLA Ops:
  0.0 36.2 %shard_map.46 = (f32[3,192,128]{2,1,0:T(8,128)S(1)}, f32[8,128]{1,0:T(8,128)S(1)}) custom-call(f32[2,32,256]{2,1,0:T(8,128)} %field_in.1, s32[256]{0:T(256)} %offsets_in.1, f32[256]{0:T(256)} %fraction_in.1, f32[2]{0:T(128)} %helm_in.1), custom_call_target="tpu_custom_call" | custom-call | tf_op jit(solution)/shard_map/pallas_call | solution.py:379
  36.2 2.2 %shard_map.47 = f32[2,32,256]{2,1,0:T(8,128)} custom-call(f32[3,192,128]{2,1,0:T(8,128)S(1)} %get-tuple-element.7.ext, f32[8,128]{1,0:T(8,128)S(1)} %get-tuple-element.8.coef), custom_call_target="tpu_custom_call" | custom-call | tf_op jit(solution)/shard_map/pallas_call | solution.py:402
